TPU v7x, 32 devices: a whole 2x2x4 slice. The times are simulated.
32 devices in a mesh: dp: 16 (over z, y, core), shard: 2 (over x).
Axes of the slice: x: 2, y: 2, z: 4, core: 2. Of those that a mesh axis runs over, the one named last changes fastest.
Arguments:
- tokens: bfloat16 [32, 512, 1024], P('dp', 'shard'), may hold values from -6 to 6
- cotangent: bfloat16 [32, 512, 1024], P('dp', 'shard'), may hold values from -6 to 6
- lengths: int32 [32], P('dp'), may hold values from 1 to 512, as said below
- entry_weight: float32 [1024, 4096], P(('dp', 'shard')), may hold values from -0.1875 to 0.1875
- output_weight: float32 [2048, 1024], P(('dp', 'shard')), may hold values from -0.5 to 0.5
- gate_weight: float32 [1024, 6144], P(('dp', 'shard')), may hold values from -0.1875 to 0.1875
- down_weight: float32 [3072, 1024], P(('dp', 'shard')), may hold values from -0.21875 to 0.21875
- entry_first: float32 [1024, 4096], P(('dp', 'shard')), may hold values from -80 to 80
- output_first: float32 [2048, 1024], P(('dp', 'shard')), may hold values from -16 to 16
- gate_first: float32 [1024, 6144], P(('dp', 'shard')), may hold values from -48 to 48
- down_first: float32 [3072, 1024], P(('dp', 'shard')), may hold values from -48 to 48
- entry_second: float32 [1024, 4096], P(('dp', 'shard')), may hold values from 655.36 to 2621.44
- output_second: float32 [2048, 1024], P(('dp', 'shard')), may hold values from 26.2144 to 104.8576
- gate_second: float32 [1024, 6144], P(('dp', 'shard')), may hold values from 278.528 to 1114.112
- down_second: float32 [3072, 1024], P(('dp', 'shard')), may hold values from 235.9296 to 943.7184
- gains: float32 [2304], replicated, may hold values from 0.5 to 1.5
- gains_first: float32 [2304], replicated, may hold values from -224 to 224
- gains_second: float32 [2304], replicated, may hold values from 5242.88 to 20971.52
Outputs:
- block_out: bfloat16 [32, 512, 1024], P('dp', 'shard')
- token_grad: float32 [32, 512, 1024], P('dp', 'shard')
- new_entry: float32 [1024, 4096], P(('dp', 'shard'))
- new_entry_first: float32 [1024, 4096], P(('dp', 'shard'))
- new_entry_second: float32 [1024, 4096], P(('dp', 'shard'))
- new_output: float32 [2048, 1024], P(('dp', 'shard'))
- new_output_first: float32 [2048, 1024], P(('dp', 'shard'))
- new_output_second: float32 [2048, 1024], P(('dp', 'shard'))
- new_gate: float32 [1024, 6144], P(('dp', 'shard'))
- new_gate_first: float32 [1024, 6144], P(('dp', 'shard'))
- new_gate_second: float32 [1024, 6144], P(('dp', 'shard'))
- new_down: float32 [3072, 1024], P(('dp', 'shard'))
- new_down_first: float32 [3072, 1024], P(('dp', 'shard'))
- new_down_second: float32 [3072, 1024], P(('dp', 'shard'))
- new_gains: float32 [2304], replicated
- new_gains_first: float32 [2304], replicated
- new_gains_second: float32 [2304], replicated
Inputs may be any that keep to these rules, and one draw needn't show every extreme that they name: `lengths`: in each aligned block of 2 sequences (the sequences of one data group) one has length exactly 512.
All inputs are finite; a program needn't handle non-finite values.
Results may differ from a plain program's by a relative error of at most 0.012.
The roundings to bfloat16 on the way count: a program that leaves them out, or rounds other values in their place, can miss the bound.
Values may be sent and summed in bfloat16 or wider, within the bound.
No kernel may reach another device: no remote copies, remote signals or barrier semaphores. Data moves between devices by JAX's collectives and lax.ppermute only.
A program may use at most 320 MiB of HBM per device.

v0:
```python
import jax
import jax.numpy as jnp
from jax import lax
from jax.sharding import PartitionSpec as P

D = 1024
HEADS = 16
KV_HEADS = 8
HEAD_DIM = 128
FF = 3072
STEP = 10


EPS = 1e-06
THETA = 1000000.0
NEG = -1e30
BETA_ONE = 0.9
BETA_TWO = 0.95
ADAM_EPS = 1e-08
DECAY = 0.1
RATE_MATRIX = 0.03
RATE_OUTPUT = 0.06
RATE_GAIN = 0.25


def norm_rows(values, gain):
    factor = lax.rsqrt(jnp.mean(values * values, axis=-1, keepdims=True) + EPS)
    return (values * factor * gain, factor)


def norm_back(values, factor, gain, incoming):
    normal = values * factor
    scaled = incoming * gain
    inner = jnp.mean(scaled * normal, axis=-1, keepdims=True)
    return (factor * (scaled - normal * inner), incoming * normal)


def rotate(values, cosine, sine, direction):
    half = values.shape[-1] // 2
    leading = values[..., :half]
    trailing = values[..., half:]
    return jnp.concatenate(
        [
            leading * cosine - direction * trailing * sine,
            trailing * cosine + direction * leading * sine,
        ],
        axis=-1,
    )


def angles(positions):
    freqs = THETA ** (-(jnp.arange(HEAD_DIM // 2).astype(jnp.float32) * 2.0) / HEAD_DIM)
    turned = positions.astype(jnp.float32)[:, None] * freqs[None, :]
    return (jnp.cos(turned), jnp.sin(turned))


def adam(weight, moment_one, moment_two, grad, rate, decay):
    new_one = BETA_ONE * moment_one + (1.0 - BETA_ONE) * grad
    new_two = BETA_TWO * moment_two + (1.0 - BETA_TWO) * grad * grad
    ratio = (
        new_one / (1.0 - BETA_ONE**STEP) / (jnp.sqrt(new_two / (1.0 - BETA_TWO**STEP)) + ADAM_EPS)
    )
    return (weight - rate * (ratio + decay * weight), new_one, new_two)


def reduce_pair(grad_left, grad_right):
    replicas = lax.axis_size("dp")
    members = lax.axis_size("shard")
    owners = replicas * members
    left_cols = grad_left.shape[1]
    right_cols = grad_right.shape[1]
    left_rows = grad_left.shape[0] // owners
    right_rows = grad_right.shape[0] // owners
    left_owned, right_owned = (
        lax.psum_scatter(grad_left.reshape(-1), ("dp", "shard"), scatter_dimension=0, tiled=True),
        lax.psum_scatter(grad_right.reshape(-1), ("dp", "shard"), scatter_dimension=0, tiled=True),
    )
    return (left_owned.reshape(left_rows, left_cols), right_owned.reshape(right_rows, right_cols))


def on_device(
    tokens,
    cotangent,
    lengths,
    entry_weight,
    output_weight,
    gate_weight,
    down_weight,
    entry_first,
    output_first,
    gate_first,
    down_first,
    entry_second,
    output_second,
    gate_second,
    down_second,
    gains,
    gains_first,
    gains_second,
):
    seq_count = tokens.shape[0]
    local_len = tokens.shape[1]
    group_size = HEADS // KV_HEADS
    query_cols = HEADS * HEAD_DIM
    key_cols = KV_HEADS * HEAD_DIM
    scale = HEAD_DIM ** (-0.5)
    bf16 = jnp.bfloat16
    single_float = jnp.float32
    entry_low = entry_weight.astype(bf16)
    output_low = output_weight.astype(bf16)
    gate_low = gate_weight.astype(bf16)
    down_low = down_weight.astype(bf16)
    entry_weight_whole, output_weight_whole, gate_weight_whole, down_weight_whole = (
        lax.all_gather(entry_low, ("dp", "shard"), axis=0, tiled=True),
        lax.all_gather(output_low, ("dp", "shard"), axis=0, tiled=True),
        lax.all_gather(gate_low, ("dp", "shard"), axis=0, tiled=True),
        lax.all_gather(down_low, ("dp", "shard"), axis=0, tiled=True),
    )
    g_attn = gains[:D]
    g_mlp = gains[D : 2 * D]
    g_query = gains[2 * D : 2 * D + HEAD_DIM]
    g_key = gains[2 * D + HEAD_DIM :]
    positions = lax.axis_index("shard") * local_len + jnp.arange(local_len)
    cosine, sine = angles(positions)
    cos_four = cosine[None, :, None, :]
    sin_four = sine[None, :, None, :]
    live = positions[None, :] < lengths[:, None]
    inputs = tokens.astype(single_float)
    normed_one, factor_one = norm_rows(inputs, g_attn)
    normed_reduced = normed_one.astype(bf16)
    projected = jnp.dot(normed_reduced, entry_weight_whole, preferred_element_type=single_float)
    query_raw = projected[..., :query_cols].reshape(seq_count, local_len, HEADS, HEAD_DIM)
    key_raw = projected[..., query_cols : query_cols + key_cols].reshape(
        seq_count, local_len, KV_HEADS, HEAD_DIM
    )
    value_low = projected[..., query_cols + key_cols :].astype(bf16)
    query_normed, query_factor = norm_rows(query_raw, g_query)
    key_normed, key_factor = norm_rows(key_raw, g_key)
    query_rot = rotate(query_normed, cos_four, sin_four, 1.0).astype(bf16)
    key_rot = rotate(key_normed, cos_four, sin_four, 1.0).astype(bf16)
    query_grouped = query_rot.reshape(seq_count, local_len, KV_HEADS, group_size, HEAD_DIM)
    key_all, value_all = (
        lax.all_gather(
            key_rot.reshape(seq_count, local_len, key_cols), "shard", axis=1, tiled=True
        ),
        lax.all_gather(value_low, "shard", axis=1, tiled=True),
    )
    whole_len = key_all.shape[1]
    key_heads = key_all.reshape(seq_count, whole_len, KV_HEADS, HEAD_DIM)
    value_heads = value_all.reshape(seq_count, whole_len, KV_HEADS, HEAD_DIM)
    key_place = jnp.arange(whole_len)
    allowed = (key_place[None, None, :] <= positions[None, :, None]) & (
        key_place[None, None, :] < lengths[:, None, None]
    )
    raw = (
        jnp.einsum(
            "sqgrd,skgd->sgrqk", query_grouped, key_heads, preferred_element_type=single_float
        )
        * scale
    )
    scores = jnp.where(allowed[:, None, None], raw, NEG)
    probs = jax.nn.softmax(scores, axis=-1)
    probs_low = probs.astype(bf16)
    context = jnp.einsum(
        "sgrqk,skgd->sqgrd", probs_low, value_heads, preferred_element_type=single_float
    )
    context_reduced = context.reshape(seq_count, local_len, query_cols).astype(bf16)
    attended = jnp.dot(context_reduced, output_weight_whole, preferred_element_type=single_float)
    middle = inputs + attended
    normed_two, factor_two = norm_rows(middle, g_mlp)
    second_normed_reduced = normed_two.astype(bf16)
    both = jnp.dot(second_normed_reduced, gate_weight_whole, preferred_element_type=single_float)
    gate_val = both[..., :FF]
    up_val = both[..., FF:]
    sigmoid_val = jax.nn.sigmoid(gate_val)
    silu_val = gate_val * sigmoid_val
    hidden_reduced = (silu_val * up_val).astype(bf16)
    mlp_out = jnp.dot(hidden_reduced, down_weight_whole, preferred_element_type=single_float)
    block_out = jnp.where(live[..., None], middle + mlp_out, 0.0).astype(bf16)
    backward_reduced = jnp.where(live[..., None], cotangent, jnp.zeros_like(cotangent))
    down_gradient = jnp.einsum(
        "goj,gob->jb", hidden_reduced, backward_reduced, preferred_element_type=single_float
    )
    hidden_gradient = jnp.einsum(
        "bov,gv->bog", backward_reduced, down_weight_whole, preferred_element_type=single_float
    )
    d_gate = hidden_gradient * up_val * sigmoid_val * (1.0 + gate_val * (1.0 - sigmoid_val))
    d_up = hidden_gradient * silu_val
    combined_gradient = jnp.concatenate([d_gate, d_up], axis=-1).astype(bf16)
    gate_gradient = jnp.einsum(
        "mit,mib->tb", second_normed_reduced, combined_gradient, preferred_element_type=single_float
    )
    owned_gate, owned_down = reduce_pair(gate_gradient, down_gradient)
    second_normed_gradient = jnp.einsum(
        "nar,yr->nay", combined_gradient, gate_weight_whole, preferred_element_type=single_float
    )
    d_middle_norm, mlp_gain_terms = norm_back(middle, factor_two, g_mlp, second_normed_gradient)
    d_middle = backward_reduced.astype(single_float) + d_middle_norm
    attention_gradient_reduced = d_middle.astype(bf16)
    output_gradient = jnp.einsum(
        "czm,czr->mr",
        context_reduced,
        attention_gradient_reduced,
        preferred_element_type=single_float,
    )
    context_gradient = jnp.einsum(
        "xoj,gj->xog",
        attention_gradient_reduced,
        output_weight_whole,
        preferred_element_type=single_float,
    )
    d_context_low = context_gradient.astype(bf16).reshape(
        seq_count, local_len, KV_HEADS, group_size, HEAD_DIM
    )
    d_probs = jnp.einsum(
        "sqgrd,skgd->sgrqk", d_context_low, value_heads, preferred_element_type=single_float
    )
    d_scores = probs * (d_probs - jnp.sum(probs * d_probs, axis=-1, keepdims=True))
    d_scores_low = d_scores.astype(bf16)
    d_query_rot = (
        jnp.einsum(
            "sgrqk,skgd->sqgrd", d_scores_low, key_heads, preferred_element_type=single_float
        )
        * scale
    )
    d_key_all = (
        jnp.einsum(
            "sgrqk,sqgrd->skgd", d_scores_low, query_grouped, preferred_element_type=single_float
        )
        * scale
    )
    d_value_all = jnp.einsum(
        "sgrqk,sqgrd->skgd", probs_low, d_context_low, preferred_element_type=single_float
    )
    d_key_own, d_value_own = (
        lax.psum_scatter(
            d_key_all.reshape(seq_count, whole_len, key_cols).astype(jnp.bfloat16),
            "shard",
            scatter_dimension=1,
            tiled=True,
        ).astype(jnp.float32),
        lax.psum_scatter(
            d_value_all.reshape(seq_count, whole_len, key_cols).astype(jnp.bfloat16),
            "shard",
            scatter_dimension=1,
            tiled=True,
        ).astype(jnp.float32),
    )
    d_query_turned = rotate(
        d_query_rot.reshape(seq_count, local_len, HEADS, HEAD_DIM), cos_four, sin_four, -1.0
    )
    d_key_turned = rotate(
        d_key_own.reshape(seq_count, local_len, KV_HEADS, HEAD_DIM), cos_four, sin_four, -1.0
    )
    d_query_raw, query_gain_terms = norm_back(query_raw, query_factor, g_query, d_query_turned)
    d_key_raw, key_gain_terms = norm_back(key_raw, key_factor, g_key, d_key_turned)
    projected_gradient = jnp.concatenate(
        [
            d_query_raw.reshape(seq_count, local_len, query_cols),
            d_key_raw.reshape(seq_count, local_len, key_cols),
            d_value_own,
        ],
        axis=-1,
    ).astype(bf16)
    entry_gradient = jnp.einsum(
        "mit,mib->tb", normed_reduced, projected_gradient, preferred_element_type=single_float
    )
    owned_entry, owned_output = reduce_pair(entry_gradient, output_gradient)
    first_normed_gradient = jnp.einsum(
        "nar,yr->nay", projected_gradient, entry_weight_whole, preferred_element_type=single_float
    )
    d_inputs_norm, attn_gain_terms = norm_back(inputs, factor_one, g_attn, first_normed_gradient)
    token_grad = d_middle + d_inputs_norm
    gain_terms = jnp.concatenate(
        [
            jnp.sum(attn_gain_terms, axis=(0, 1)),
            jnp.sum(mlp_gain_terms, axis=(0, 1)),
            jnp.sum(query_gain_terms, axis=(0, 1, 2)),
            jnp.sum(key_gain_terms, axis=(0, 1, 2)),
        ]
    )
    grad_gains = lax.psum(gain_terms, ("dp", "shard"))
    new_entry, new_entry_first, new_entry_second = adam(
        entry_weight, entry_first, entry_second, owned_entry, RATE_MATRIX, DECAY
    )
    new_output, new_output_first, new_output_second = adam(
        output_weight, output_first, output_second, owned_output, RATE_OUTPUT, DECAY
    )
    new_gate, new_gate_first, new_gate_second = adam(
        gate_weight, gate_first, gate_second, owned_gate, RATE_MATRIX, DECAY
    )
    new_down, new_down_first, new_down_second = adam(
        down_weight, down_first, down_second, owned_down, RATE_MATRIX, DECAY
    )
    new_gains, new_gains_first, new_gains_second = adam(
        gains, gains_first, gains_second, grad_gains, RATE_GAIN, 0.0
    )
    return (
        block_out,
        token_grad,
        new_entry,
        new_entry_first,
        new_entry_second,
        new_output,
        new_output_first,
        new_output_second,
        new_gate,
        new_gate_first,
        new_gate_second,
        new_down,
        new_down_first,
        new_down_second,
        new_gains,
        new_gains_first,
        new_gains_second,
    )


def solution(mesh):
    return jax.shard_map(
        on_device,
        mesh=mesh,
        in_specs=(
            P("dp", "shard", None),
            P("dp", "shard", None),
            P("dp"),
            P(("dp", "shard"), None),
            P(("dp", "shard"), None),
            P(("dp", "shard"), None),
            P(("dp", "shard"), None),
            P(("dp", "shard"), None),
            P(("dp", "shard"), None),
            P(("dp", "shard"), None),
            P(("dp", "shard"), None),
            P(("dp", "shard"), None),
            P(("dp", "shard"), None),
            P(("dp", "shard"), None),
            P(("dp", "shard"), None),
            P(),
            P(),
            P(),
        ),
        out_specs=(
            P("dp", "shard", None),
            P("dp", "shard", None),
            P(("dp", "shard"), None),
            P(("dp", "shard"), None),
            P(("dp", "shard"), None),
            P(("dp", "shard"), None),
            P(("dp", "shard"), None),
            P(("dp", "shard"), None),
            P(("dp", "shard"), None),
            P(("dp", "shard"), None),
            P(("dp", "shard"), None),
            P(("dp", "shard"), None),
            P(("dp", "shard"), None),
            P(("dp", "shard"), None),
            P(),
            P(),
            P(),
        ),
        check_vma=False,
    )
```

profile of v0, /device:TPU:0, one launch (start us, length us, event | category | flops | bytes accessed | tf_op | source)
XLA Modules:
  0.0 1561.2 jit_solution(7715196508698867796)
XLA Ops:
  11.3 80.3 %all-gather.7.cloned.1.call-done = bf16[1024,4096]{1,0:T(8,128)(2,1)} async-done(((bf16[32,4096]{1,0:T(8,128)(2,1)}), bf16[1024,4096]{1,0:T(8,128)(2,1)}) %all-gather.7.cloned.1.call-update) | async-done | bytes 8388624 | tf_op jit(solution)/shard_map/all_gather | solution.py:114
  91.6 7.4 fusion.11
  140.2 29.7 %all-gather.11.cloned.1.call-done = bf16[2,512,1024]{1,2,0:T(8,128)(2,1)} async-done(((bf16[2,256,1024]{1,2,0:T(8,128)(2,1)}), bf16[2,512,1024]{1,2,0:T(8,128)(2,1)}) %all-gather.11.cloned.1.call-update) | async-done | bytes 2097168 | tf_op jit(solution)/shard_map/all_gather | solution.py:143
  169.9 11.7 fusion.91
  181.6 9.5 fusion.48
  191.1 44.3 %all-gather.13.cloned.1.call-done = bf16[2048,1024]{1,0:T(8,128)(2,1)} async-done(((bf16[64,1024]{1,0:T(8,128)(2,1)}), bf16[2048,1024]{1,0:T(8,128)(2,1)}) %all-gather.13.cloned.1.call-update) | async-done | bytes 4194320 | tf_op jit(solution)/shard_map/all_gather | solution.py:115
  235.4 5.3 multiply_reduce_fusion.6
  240.7 92.6 %all-gather.15.cloned.1.call-done = bf16[1024,6144]{1,0:T(8,128)(2,1)} async-done(((bf16[32,6144]{1,0:T(8,128)(2,1)}), bf16[1024,6144]{1,0:T(8,128)(2,1)}) %all-gather.15.cloned.1.call-update) | async-done | bytes 12582928 | tf_op jit(solution)/shard_map/all_gather | solution.py:116
  333.3 14.6 fusion.7
  347.9 56.6 %all-gather.17.cloned.1.call-done = bf16[3072,1024]{1,0:T(8,128)(2,1)} async-done(((bf16[96,1024]{1,0:T(8,128)(2,1)}), bf16[3072,1024]{1,0:T(8,128)(2,1)}) %all-gather.17.cloned.1.call-update) | async-done | bytes 6291472 | tf_op jit(solution)/shard_map/all_gather | solution.py:117
  404.5 12.6 multiply_convert_fusion.1
  417.1 14.4 multiply_reduce_fusion.3
  443.0 12.7 fusion.1
  455.7 11.5 fusion.3
  467.2 9.5 fusion.22
  476.8 11.3 bitcast_convert_fusion
  492.1 5.3 convolution_multiply_fusion
  504.5 4.9 copy.141
  514.1 16.5 %multiply_reduce_fusion.1 = (f32[2,256,16]{2,1,0:T(8,128)S(1)}, f32[2,256,16,128]{3,2,1,0:T(8,128)}) fusion(f32[128]{0:T(128)S(1)} %copy-done.48, f32[2,256,16]{2,1,0:T(8,128)S(1)} %copy-done.14, f32[2,256,16,64]{3,2,1,0:T(8,128)S(1)} %get-tuple-element.52, f32[2,256,16,64]{3,2,1,0:T(8,128)S(1)} %get-tuple-element.51, f32[2,256,16,128]{3,2,1,0:T(8,128)S(1)} %bitcast.177), kind=kLoop, calls=%fused_computation.48 | loop fusion | flops 5234688 | bytes 12648960 | tf_op jit(solution)/shard_map/reduce_sum | solution.py:34
  547.7 5.4 copy.150
  553.2 15.2 convolution_bitcast_fusion
  568.4 21.2 %copy.151 = f32[128,48,8,128]{3,1,2,0:T(8,128)} copy(f32[128,48,8,128]{3,2,1,0:T(8,128)} %convolution_bitcast_fusion) | data formatting | bytes 50331648
  589.5 6.6 convolution_bitcast_fusion.2
  596.1 12.3 copy.152
  608.4 8.5 multiply_reduce_fusion
  637.5 5.6 multiply_reduce_fusion.2
  643.1 6.9 convolution_bitcast_fusion.1
  650.0 7.2 copy.149
  657.3 8.3 select_convert_fusion
  665.7 9.7 fusion.44
  675.4 41.1 %psum.7 = f32[2304]{0:T(1024)S(1)} all-reduce(f32[2304]{0:T(1024)S(1)} %pad_maximum_fusion.10), channel_id=1, replica_groups=mesh['dp'=16,'shard'=2] {'dp','shard'}, use_global_device_ids=true, to_apply=%region_23.24 | all-reduce | flops 2304 | bytes 18432 | tf_op jit(solution)/shard_map/psum | solution.py:282
  720.7 821.4 %all-reduce.7.cloned.1.call-done = (f32[4194304]{0:T(1024)}, f32[2097152]{0:T(1024)}, f32[6291456]{0:T(1024)}, f32[3145728]{0:T(1024)}) async-done(((f32[4194304]{0:T(1024)}, f32[2097152]{0:T(1024)}, f32[6291456]{0:T(1024)}, f32[3145728]{0:T(1024)}), (f32[4194304]{0:T(1024)}, f32[2097152]{0:T(1024)}, f32[6291456]{0:T(1024)}, f32[3145728]{0:T(1024)})) %all-reduce.7.cloned.1.call-update) | async-done | bytes 62914576
  (213 shorter events, 126.4 us)
Async XLA Ops:
  7.2 84.4 %all-gather.7.cloned.1.call-start = ((), (), s32[]{:S(2)}) async-start(), calls=%async_computation.2 | async-start | bytes 8650752 | tf_op jit(solution)/shard_map/all_gather | solution.py:114
  9.0 127.5 %all-gather.9.cloned.1.call-start = ((), (), s32[]{:S(2)}) async-start(), calls=%async_computation.3 | async-start | bytes 3145728 | tf_op jit(solution)/shard_map/all_gather | solution.py:146
  10.6 88.4 %copy-start.40 = (f32[2,256]{1,0:T(2,128)}, f32[2,256]{1,0:T(2,128)S(1)}, u32[]{:S(2)}) copy-start(f32[2,256]{1,0:T(2,128)S(1)} %add_rsqrt_fusion.3) | copy-start | bytes 6148
  11.3 87.7 %copy-start.34 = (f32[1024]{0:T(1024)}, f32[1024]{0:T(1024)S(1)}, u32[]{:S(2)}) copy-start(f32[1024]{0:T(1024)S(1)} %get-tuple-element.64) | copy-start | bytes 12292
  103.4 66.5 %all-gather.11.cloned.1.call-start = ((), (), s32[]{:S(2)}) async-start(), calls=%async_computation.4 | async-start | bytes 3145728 | tf_op jit(solution)/shard_map/all_gather | solution.py:143
  104.3 8.6 copy-start.49
  104.3 14.4 copy-start.47
  105.5 14.7 copy-start.18
  106.6 17.7 %copy-start.15 = (f32[2,256,8]{2,1,0:T(8,128)}, f32[2,256,8]{2,1,0:T(8,128)S(1)}, u32[]{:S(2)}) copy-start(f32[2,256,8]{2,1,0:T(8,128)S(1)} %add_rsqrt_fusion.1) | copy-start | bytes 49156
  110.3 125.2 %all-gather.13.cloned.1.call-start = ((), (), s32[]{:S(2)}) async-start(), calls=%async_computation.5 | async-start | bytes 4325376 | tf_op jit(solution)/shard_map/all_gather | solution.py:115
  111.0 222.3 %all-gather.15.cloned.1.call-start = ((), (), s32[]{:S(2)}) async-start(), calls=%async_computation.6 | async-start | bytes 12976128 | tf_op jit(solution)/shard_map/all_gather | solution.py:116
  111.9 292.6 %all-gather.17.cloned.1.call-start = ((), (), s32[]{:S(2)}) async-start(), calls=%async_computation.7 | async-start | bytes 6488064 | tf_op jit(solution)/shard_map/all_gather | solution.py:117
  112.7 504.2 %reduce-scatter.3.cloned.1.call-start = ((), (), s32[]{:S(2)}) async-start(), calls=%async_computation.8 | async-start | bytes 3145728 | tf_op jit(solution)/shard_map/reduce_scatter | solution.py:236
  118.7 10.3 copy-start.13
  122.3 47.6 %copy-start.8 = (bf16[2,256,16,64]{3,1,2,0:T(8,128)(2,1)}, bf16[2,256,16,64]{3,1,2,0:T(8,128)(2,1)S(1)}, u32[]{:S(2)}) copy-start(bf16[2,256,16,64]{3,1,2,0:T(8,128)(2,1)S(1)} %copy.99) | copy-start | bytes 3145732
  181.6 53.9 %copy-start.6 = (bf16[2,256,1024]{2,1,0:T(8,128)(2,1)S(1)}, bf16[2,256,1024]{2,1,0:T(8,128)(2,1)}, u32[]{:S(2)}) copy-start(bf16[2,256,1024]{2,1,0:T(8,128)(2,1)} %param.18) | copy-start | bytes 3145732
  333.3 71.2 %copy-start.26 = (bf16[2,256,1024]{2,1,0:T(8,128)(2,1)S(1)}, bf16[2,256,1024]{2,1,0:T(8,128)(2,1)}, u32[]{:S(2)}) copy-start(bf16[2,256,1024]{2,1,0:T(8,128)(2,1)} %param.19) | copy-start | bytes 3145732
  467.2 9.5 copy-start
  476.7 166.3 %reduce-scatter.5.cloned.1.call-start = ((), (), s32[]{:S(2)}) async-start(), calls=%async_computation.9 | async-start | bytes 3145728 | tf_op jit(solution)/shard_map/reduce_scatter | solution.py:242
  553.1 989.0 %all-reduce.7.cloned.1.call-start = ((), (), s32[]{:S(2)}) async-start(), calls=%async_computation.10 | async-start | bytes 125829120
  568.4 21.2 %copy-start.27 = (bf16[2,256,1024]{2,1,0:T(8,128)(2,1)S(1)}, bf16[2,256,1024]{2,1,0:T(8,128)(2,1)}, u32[]{:S(2)}) copy-start(bf16[2,256,1024]{2,1,0:T(8,128)(2,1)} %param.19) | copy-start | bytes 3145732
  568.4 21.2 %copy-start.53 = (bf16[2,256,3072]{2,1,0:T(8,128)(2,1)S(1)}, bf16[2,256,3072]{2,1,0:T(8,128)(2,1)}, u32[]{:S(2)}) copy-start(bf16[2,256,3072]{2,1,0:T(8,128)(2,1)} %get-tuple-element.50) | copy-start | bytes 9437188
  596.1 12.3 copy-start.43
  637.5 5.6 copy-start.41
  657.3 8.3 copy-start.11
  657.3 8.3 copy-start.17
  657.3 8.3 copy-start.28
  665.6 9.8 copy-start.51
  665.6 50.9 %copy-start.42 = (f32[2304]{0:T(1024)S(1)}, f32[2304]{0:T(1024)}, u32[]{:S(2)}) copy-start(f32[2304]{0:T(1024)} %param.33) | copy-start | bytes 27652
  665.6 50.9 %copy-start.45 = (f32[2304]{0:T(1024)S(1)}, f32[2304]{0:T(1024)}, u32[]{:S(2)}) copy-start(f32[2304]{0:T(1024)} %param.34) | copy-start | bytes 27652
  665.6 50.9 %copy-start.46 = (f32[2304]{0:T(1024)S(1)}, f32[2304]{0:T(1024)}, u32[]{:S(2)}) copy-start(f32[2304]{0:T(1024)} %param.35) | copy-start | bytes 27652
  665.6 51.5 %copy-start.10 = (f32[2,256,1024]{2,1,0:T(8,128)S(1)}, f32[2,256,1024]{2,1,0:T(8,128)}, u32[]{:S(2)}) copy-start(f32[2,256,1024]{2,1,0:T(8,128)} %copy-done.9) | copy-start | bytes 6291460
  (33 other events, 109.5 us)
Sparse Core Ops, SparseCore 0:
  11.6 79.9 all-gather.6
  103.5 31.7 all-gather.8
  136.8 33.0 all-gather.10
  173.3 62.0 all-gather.12
  238.7 94.5 all-gather.14
  336.6 67.8 all-gather.16
  476.9 30.2 reduce-scatter.2
  553.2 30.2 reduce-scatter.4
  657.4 884.7 all-reduce.6
where the time goes:
time: 1570 us; the launch traced here: 1560 us
  waiting for transfers between devices  1130 us (72%)
  matrix products  169 us (11%)
  local copies, waits for them, and re-layouts  131 us (8%)
  other arithmetic  79.6 us (5%)
  blocking collectives  41.1 us (3%)
    unnamed x10, waiting for transfers between devices  822 us
    all_gather x1, waiting for transfers between devices, on_device(): lax.all_gather(gate_low, ('dp', 'shard'), axis=0, tiled=True)  92.6 us
    all_gather x1, waiting for transfers between devices, on_device(): lax.all_gather(entry_low, ('dp', 'shard'), axis=0, tiled=True)  80.3 us
    unnamed x123, local copies, waits for them, and re-layouts  73.7 us
    all_gather x1, waiting for transfers between devices, on_device(): lax.all_gather(down_low, ('dp', 'shard'), axis=0, tiled=True)  56.6 us
    all_gather x1, waiting for transfers between devices, on_device(): lax.all_gather(output_low, ('dp', 'shard'), axis=0, tiled=True)  44.3 us
    psum x1, blocking collectives, on_device(): grad_gains = lax.psum(gain_terms, ('dp', 'shard'))  41.1 us
  transfers between devices with their start and end apart: 9, of which 6 were waited for; matrix products, arithmetic and copies ran while one was open for 17% of the time, Pallas kernels for 0%

commit v1 on v0

--- a/solution.py
+++ b/solution.py
@@ -1,6 +1,8 @@
 import jax
 import jax.numpy as jnp
 from jax import lax
+from jax.experimental import pallas as pl
+from jax.experimental.pallas import tpu as pltpu
 from jax.sharding import PartitionSpec as P
 
 D = 1024
@@ -78,7 +80,214 @@
     return (left_owned.reshape(left_rows, left_cols), right_owned.reshape(right_rows, right_cols))
 
 
-def on_device(
+class Grid:
+    def __init__(self, replicas):
+        self.deep = replicas // 4
+        index = lax.axis_index("dp")
+        self.z = index // 4
+        self.y = (index // 2) % 2
+        self.c = index % 2
+        self.x = lax.axis_index("shard")
+
+    def pairs(self, turn):
+        places = [
+            (z, y, c, x)
+            for z in range(self.deep)
+            for y in range(2)
+            for c in range(2)
+            for x in range(2)
+        ]
+        flat = lambda z, y, c, x: ((z * 2 + y) * 2 + c) * 2 + x
+        return [(flat(*p), flat(*turn(*p))) for p in places]
+
+    def send(self, values, turn):
+        return lax.ppermute(values, ("dp", "shard"), self.pairs(turn))
+
+    def over_x(self, values):
+        return self.send(values, lambda z, y, c, x: (z, y, c, 1 - x))
+
+    def over_y(self, values):
+        return self.send(values, lambda z, y, c, x: (z, 1 - y, c, x))
+
+    def over_core(self, values):
+        return self.send(values, lambda z, y, c, x: (z, y, 1 - c, x))
+
+    def along_z(self, values, step):
+        return self.send(values, lambda z, y, c, x: ((z + step) % self.deep, y, c, x))
+
+    def up_x(self, values):
+        flat = [p for p in self.pairs(lambda z, y, c, x: (z, y, c, 1 - x)) if p[0] % 2 == 0]
+        return lax.ppermute(values, ("dp", "shard"), flat)
+
+    def down_x(self, values):
+        flat = [p for p in self.pairs(lambda z, y, c, x: (z, y, c, 1 - x)) if p[0] % 2 == 1]
+        return lax.ppermute(values, ("dp", "shard"), flat)
+
+
+def pick(values, index, axis):
+    return lax.dynamic_index_in_dim(values, index, axis, keepdims=False)
+
+
+def place_blocks(grid, own, sibling, rows, cols):
+    deep = grid.deep
+    half = deep // 2
+    places = jnp.stack([grid.z, grid.y, grid.c, grid.x]).astype(jnp.int32)
+    spans = [(0, deep, 0, 0), (0, deep, 0, 1), (0, deep, 1, 0), (0, half, 1, 1), (half, deep, 1, 1)]
+
+    def kernel(place_ref, *refs):
+        ins, out, held, sems, sent = refs[:10], refs[10], refs[11], refs[12], refs[13]
+        z, y, c, x = [place_ref[i] for i in range(4)]
+        copies = []
+        for core in range(2):
+            for piece, (first, last, dy, dx) in enumerate(spans):
+                for step in range(first, last):
+                    zz = lax.rem(z - step + deep, deep)
+                    yy = lax.rem(y + dy, 2)
+                    cc = lax.rem(c + core, 2)
+                    xx = lax.rem(x + dx, 2)
+                    block = ((zz * 2 + yy) * 2 + cc) * 2 + xx
+                    turn = len(copies)
+                    copies.append(
+                        (
+                            pltpu.make_async_copy(
+                                ins[core * 5 + piece].at[step - first],
+                                held.at[turn],
+                                sems.at[turn],
+                            ),
+                            pltpu.make_async_copy(held.at[turn], out.at[block], sent.at[turn]),
+                        )
+                    )
+        for arrive, leave in copies:
+            arrive.start()
+        for arrive, leave in copies:
+            arrive.wait()
+            leave.start()
+        for arrive, leave in copies:
+            leave.wait()
+
+    blocks = deep * 8
+    whole = pl.pallas_call(
+        kernel,
+        out_shape=jax.ShapeDtypeStruct((blocks, rows, cols), jnp.bfloat16),
+        in_specs=[pl.BlockSpec(memory_space=pltpu.SMEM)] + [pl.BlockSpec(memory_space=pl.ANY)] * 10,
+        out_specs=pl.BlockSpec(memory_space=pl.ANY),
+        scratch_shapes=[
+            pltpu.VMEM((blocks, rows, cols), jnp.bfloat16),
+            pltpu.SemaphoreType.DMA((blocks,)),
+            pltpu.SemaphoreType.DMA((blocks,)),
+        ],
+        compiler_params=pltpu.CompilerParams(vmem_limit_bytes=blocks * rows * cols * 2 + 2**21),
+        cost_estimate=pl.CostEstimate(
+            flops=0, bytes_accessed=blocks * rows * cols * 4, transcendentals=0
+        ),
+        name="place_blocks",
+    )(places, *own, *sibling)
+    return whole.reshape(blocks * rows, cols)
+
+
+def gather_rows(grid, shard, after_column=()):
+    deep = grid.deep
+    half = deep // 2
+    rows, cols = shard.shape
+    column = jnp.stack([shard] + [grid.along_z(shard, step) for step in range(1, deep)])
+    ready = tie(column, *after_column)
+    x_column = grid.over_x(ready)
+    y_column = grid.over_y(ready)
+    first = grid.over_y(x_column[:half])
+    second = grid.over_x(y_column[half:])
+    own = (ready, x_column, y_column, first, second)
+    sibling = tuple(grid.over_core(piece) for piece in own)
+    return place_blocks(grid, own, sibling, rows, cols), (column, first, second)
+
+
+def halves(grid, values):
+    cols = values.shape[1] // 2
+    kept = lax.dynamic_slice_in_dim(values, grid.c * cols, cols, 1)
+    sent = lax.dynamic_slice_in_dim(values, (1 - grid.c) * cols, cols, 1)
+    return kept, sent
+
+
+def both_cores(grid, left, kept, sent):
+    left_all = jnp.concatenate([left, grid.over_core(left)])
+    right_all = jnp.concatenate([kept, grid.over_core(sent)])
+    return lax.dot_general(
+        left_all, right_all, (((0,), (0,)), ((), ())), preferred_element_type=jnp.float32
+    ).astype(jnp.bfloat16)
+
+
+def added(kept, arrived):
+    return (kept.astype(jnp.float32) + arrived.astype(jnp.float32)).astype(jnp.bfloat16)
+
+
+def tie(value, *after):
+    if not after:
+        return value
+
+    def kernel(*refs):
+        pass
+
+    return pl.pallas_call(
+        kernel,
+        out_shape=jax.ShapeDtypeStruct(value.shape, value.dtype),
+        in_specs=[pl.BlockSpec(memory_space=pl.ANY)] * (1 + len(after)),
+        out_specs=pl.BlockSpec(memory_space=pl.ANY),
+        input_output_aliases={0: 0},
+        cost_estimate=pl.CostEstimate(flops=0, bytes_accessed=0, transcendentals=0),
+        name="tie",
+    )(value, *after)
+
+
+def scatter_one(grid, partial, *after):
+    rows = partial.shape[0] // (grid.deep * 8)
+    blocks = partial.reshape(grid.deep, 2, 2, 2, rows, partial.shape[1])
+    first, second = blocks[:, :, 0], blocks[:, :, 1]
+    first_sent = tie(pick(first, 1 - grid.y, 1), *after)
+    second_sent = tie(pick(second, 1 - grid.x, 2), *after)
+    return (
+        added(pick(first, grid.y, 1), grid.over_y(first_sent)),
+        added(pick(second, grid.x, 2), grid.over_x(second_sent)),
+    ), (first_sent, second_sent)
+
+
+def scatter_two(grid, sums, *after):
+    first, second = sums
+    first_sent = tie(pick(first, 1 - grid.x, 1), *after)
+    second_sent = tie(pick(second, 1 - grid.y, 1), *after)
+    return jnp.stack(
+        [
+            added(pick(first, grid.x, 1), grid.over_x(first_sent)),
+            added(pick(second, grid.y, 1), grid.over_y(second_sent)),
+        ],
+        axis=1,
+    )
+
+
+def scatter_three(grid, chip):
+    total = pick(chip, grid.z, 0).astype(jnp.float32)
+    for step in range(1, grid.deep):
+        sent = pick(chip, (grid.z + step) % grid.deep, 0)
+        total = total + grid.along_z(sent, step).astype(jnp.float32)
+    kept = pick(total, grid.c, 0)
+    arrived = grid.over_core(pick(total, 1 - grid.c, 0))
+    return jnp.where(
+        grid.c == 0,
+        jnp.concatenate([kept, arrived], axis=1),
+        jnp.concatenate([arrived, kept], axis=1),
+    )
+
+
+def sum_all(grid, values):
+    values = values + grid.over_core(values)
+    values = values + grid.over_x(values)
+    values = values + grid.over_y(values)
+    step = 1
+    while step < grid.deep:
+        values = values + grid.send(values, lambda z, y, c, x: (z ^ step, y, c, x))
+        step *= 2
+    return values
+
+
+def on_device_general(
     tokens,
     cotangent,
     lengths,
@@ -316,6 +525,484 @@
     )
 
 
+VMEM_LIMIT = 40 * 2**20
+
+
+def rope_rows(values, cosine, sine):
+    return values * cosine + pltpu.roll(values, HEAD_DIM // 2, 1) * sine
+
+
+def project_heads(normed, weight, first_block, turned_blocks, plain_blocks, cosine, sine, gain):
+    slots, width = normed.shape
+    wide = 2 * HEAD_DIM
+    blocks = turned_blocks + plain_blocks
+
+    def kernel(normed_ref, weight_ref, cos_ref, sin_ref, gain_ref, raw_ref, low_ref):
+        step = pl.program_id(0)
+        block = jnp.dot(normed_ref[...], weight_ref[...], preferred_element_type=jnp.float32)
+
+        def plain():
+            low_ref[...] = block.astype(jnp.bfloat16)
+
+        def turned():
+            raw_ref[...] = block
+            for head in range(2):
+                part = block[:, head * HEAD_DIM : (head + 1) * HEAD_DIM]
+                factor = lax.rsqrt(jnp.mean(part * part, axis=-1, keepdims=True) + EPS)
+                rows = rope_rows(part * factor * gain_ref[...], cos_ref[...], sin_ref[...])
+                low_ref[:, head * HEAD_DIM : (head + 1) * HEAD_DIM] = rows.astype(jnp.bfloat16)
+
+        if plain_blocks:
+            pl.when(step >= turned_blocks)(plain)
+            pl.when(step < turned_blocks)(turned)
+        else:
+            turned()
+
+    return pl.pallas_call(
+        kernel,
+        grid=(blocks,),
+        out_shape=(
+            jax.ShapeDtypeStruct((slots, turned_blocks * wide), jnp.float32),
+            jax.ShapeDtypeStruct((slots, blocks * wide), jnp.bfloat16),
+        ),
+        in_specs=[
+            pl.BlockSpec((slots, width), lambda j: (0, 0)),
+            pl.BlockSpec((width, wide), lambda j: (0, first_block + j)),
+            pl.BlockSpec((slots, HEAD_DIM), lambda j: (0, 0)),
+            pl.BlockSpec((slots, HEAD_DIM), lambda j: (0, 0)),
+            pl.BlockSpec((1, HEAD_DIM), lambda j: (0, 0)),
+        ],
+        out_specs=(
+            pl.BlockSpec((slots, wide), lambda j: (0, jnp.minimum(j, turned_blocks - 1))),
+            pl.BlockSpec((slots, wide), lambda j: (0, j)),
+        ),
+        compiler_params=pltpu.CompilerParams(vmem_limit_bytes=VMEM_LIMIT),
+        cost_estimate=pl.CostEstimate(
+            flops=8 * slots * width * blocks * wide,
+            bytes_accessed=12 * 2**20,
+            transcendentals=0,
+        ),
+        name="project_heads",
+    )(normed, weight, cosine, sine, gain)
+
+
+def masked_weights(query, key, places, span, shard, length, own):
+    scores = lax.dot_general(
+        query, key, (((1,), (1,)), ((), ())), preferred_element_type=jnp.float32
+    ) * (HEAD_DIM ** (-0.5))
+    slot, key_slot = places
+    if own:
+        allowed = (key_slot <= slot) & (key_slot + shard * span < length)
+    else:
+        allowed = (key_slot + (shard - 1) * span < length) & (shard > 0)
+    return jnp.where(allowed, jnp.exp(scores), 0.0)
+
+
+def attend(query, low, other, lengths, shard, seqs, span):
+    slots = seqs * span
+    wide = 2 * HEAD_DIM
+
+    def kernel(len_ref, place_ref, query_ref, key_ref, value_ref, key_far, value_far, out_ref):
+        length, here = len_ref[pl.program_id(0)], place_ref[0]
+        places = [lax.broadcasted_iota(jnp.int32, (span, span), axis) for axis in (0, 1)]
+        for head in range(2):
+            query = query_ref[:, head * HEAD_DIM : (head + 1) * HEAD_DIM]
+            near = masked_weights(query, key_ref[...], places, span, here, length, True)
+            far = masked_weights(query, key_far[...], places, span, here, length, False)
+            total = jnp.sum(near, axis=-1, keepdims=True) + jnp.sum(far, axis=-1, keepdims=True)
+            inverse = 1.0 / total
+            context = jnp.dot(
+                (near * inverse).astype(jnp.bfloat16),
+                value_ref[...],
+                preferred_element_type=jnp.float32,
+            ) + jnp.dot(
+                (far * inverse).astype(jnp.bfloat16),
+                value_far[...],
+                preferred_element_type=jnp.float32,
+            )
+            out_ref[:, head * HEAD_DIM : (head + 1) * HEAD_DIM] = context.astype(jnp.bfloat16)
+
+    block = lambda offset: pl.BlockSpec((span, HEAD_DIM), lambda s, g: (s, offset + g))
+    return pl.pallas_call(
+        kernel,
+        grid=(seqs, KV_HEADS),
+        out_shape=jax.ShapeDtypeStruct((slots, HEADS * HEAD_DIM), jnp.bfloat16),
+        in_specs=[
+            pl.BlockSpec(memory_space=pltpu.SMEM),
+            pl.BlockSpec(memory_space=pltpu.SMEM),
+            pl.BlockSpec((span, wide), lambda s, g: (s, g)),
+            block(0),
+            block(KV_HEADS),
+            block(0),
+            block(KV_HEADS),
+        ],
+        out_specs=pl.BlockSpec((span, wide), lambda s, g: (s, g)),
+        compiler_params=pltpu.CompilerParams(vmem_limit_bytes=VMEM_LIMIT),
+        cost_estimate=pl.CostEstimate(
+            flops=8 * slots * span * HEADS * HEAD_DIM,
+            bytes_accessed=12 * 2**20,
+            transcendentals=2 * slots * span * HEADS,
+        ),
+        name="attend",
+    )(lengths, shard, query, low, low, other, other)
+
+
+def norm_back_rows(raw, gain, incoming):
+    factor = lax.rsqrt(jnp.mean(raw * raw, axis=-1, keepdims=True) + EPS)
+    normal = raw * factor
+    scaled = incoming * gain
+    inner = jnp.mean(scaled * normal, axis=-1, keepdims=True)
+    return factor * (scaled - normal * inner), jnp.sum(incoming * normal, axis=0, keepdims=True)
+
+
+def attend_back(
+    query, low, other, raw, d_context, lengths, shard, cosine, sine, gain, seqs, span, after
+):
+    slots = seqs * span
+    wide = 2 * HEAD_DIM
+    scale = HEAD_DIM ** (-0.5)
+
+    def kernel(
+        len_ref,
+        place_ref,
+        query_ref,
+        key_ref,
+        value_ref,
+        key_far,
+        value_far,
+        raw_ref,
+        d_context_ref,
+        cos_ref,
+        sin_ref,
+        gain_ref,
+        *rest,
+    ):
+        d_query_ref, d_near_ref, d_value_ref, far_ref, far_value_ref, terms_ref = rest[-6:]
+        length, here = len_ref[pl.program_id(0)], place_ref[0]
+        places = [lax.broadcasted_iota(jnp.int32, (span, span), axis) for axis in (0, 1)]
+        keys, values = (key_ref[...], key_far[...]), (value_ref[...], value_far[...])
+        d_keys, d_values = [0.0, 0.0], [0.0, 0.0]
+        terms = 0.0
+        for head in range(2):
+            cols = slice(head * HEAD_DIM, (head + 1) * HEAD_DIM)
+            query, d_out = query_ref[:, cols], d_context_ref[:, cols]
+            weights = [
+                masked_weights(query, keys[i], places, span, here, length, i == 0)
+                for i in range(2)
+            ]
+            total = sum(jnp.sum(w, axis=-1, keepdims=True) for w in weights)
+            inverse = 1.0 / total
+            probs = [w * inverse for w in weights]
+            d_probs = [
+                lax.dot_general(
+                    d_out, values[i], (((1,), (1,)), ((), ())), preferred_element_type=jnp.float32
+                )
+                for i in range(2)
+            ]
+            inner = sum(jnp.sum(p * d, axis=-1, keepdims=True) for p, d in zip(probs, d_probs))
+            d_query = 0.0
+            for i in range(2):
+                d_scores = (probs[i] * (d_probs[i] - inner)).astype(jnp.bfloat16)
+                turn = (((0,), (0,)), ((), ()))
+                d_query += jnp.dot(d_scores, keys[i], preferred_element_type=jnp.float32)
+                d_keys[i] += lax.dot_general(
+                    d_scores, query, turn, preferred_element_type=jnp.float32
+                )
+                d_values[i] += lax.dot_general(
+                    probs[i].astype(jnp.bfloat16), d_out, turn, preferred_element_type=jnp.float32
+                )
+            turned = rope_rows(d_query * scale, cos_ref[...], -sin_ref[...])
+            d_raw, gain_term = norm_back_rows(raw_ref[:, cols], gain_ref[...], turned)
+            d_query_ref[:, cols] = d_raw.astype(jnp.bfloat16)
+            terms += gain_term
+        d_near_ref[...] = d_keys[0] * scale
+        d_value_ref[...] = d_values[0]
+        far_ref[...] = (d_keys[1] * scale).astype(jnp.bfloat16)
+        far_value_ref[...] = d_values[1].astype(jnp.bfloat16)
+
+        @pl.when((pl.program_id(0) == 0) & (pl.program_id(1) == 0))
+        def _():
+            terms_ref[...] = jnp.zeros_like(terms_ref)
+
+        terms_ref[...] += terms
+
+    block = lambda offset: pl.BlockSpec((span, HEAD_DIM), lambda s, g: (s, offset + g))
+    pair = pl.BlockSpec((span, wide), lambda s, g: (s, g))
+    table = pl.BlockSpec((span, HEAD_DIM), lambda s, g: (0, 0))
+    key_shape = (slots, KV_HEADS * HEAD_DIM)
+    return pl.pallas_call(
+        kernel,
+        grid=(seqs, KV_HEADS),
+        out_shape=(
+            jax.ShapeDtypeStruct((slots, HEADS * HEAD_DIM), jnp.bfloat16),
+            jax.ShapeDtypeStruct(key_shape, jnp.float32),
+            jax.ShapeDtypeStruct(key_shape, jnp.float32),
+            jax.ShapeDtypeStruct(key_shape, jnp.bfloat16),
+            jax.ShapeDtypeStruct(key_shape, jnp.bfloat16),
+            jax.ShapeDtypeStruct((1, HEAD_DIM), jnp.float32),
+        ),
+        in_specs=[
+            pl.BlockSpec(memory_space=pltpu.SMEM),
+            pl.BlockSpec(memory_space=pltpu.SMEM),
+            pair,
+            block(0),
+            block(KV_HEADS),
+            block(0),
+            block(KV_HEADS),
+            pair,
+            pair,
+            table,
+            table,
+            pl.BlockSpec((1, HEAD_DIM), lambda s, g: (0, 0)),
+        ]
+        + [pl.BlockSpec(memory_space=pl.ANY)] * len(after),
+        out_specs=(
+            pair,
+            block(0),
+            block(0),
+            block(0),
+            block(0),
+            pl.BlockSpec((1, HEAD_DIM), lambda s, g: (0, 0)),
+        ),
+        compiler_params=pltpu.CompilerParams(vmem_limit_bytes=VMEM_LIMIT),
+        cost_estimate=pl.CostEstimate(
+            flops=20 * slots * span * HEADS * HEAD_DIM,
+            bytes_accessed=24 * 2**20,
+            transcendentals=2 * slots * span * HEADS,
+        ),
+        name="attend_back",
+    )(lengths, shard, query, low, low, other, other, raw, d_context, cosine, sine, gain, *after)
+
+
+def key_value_back(raw, d_key, d_value, key_arrived, value_arrived, cosine, sine, gain, after):
+    slots = raw.shape[0]
+
+    def kernel(
+        raw_ref, key_ref, value_ref, key_more, value_more, cos_ref, sin_ref, gain_ref, *rest
+    ):
+        out_ref, terms_ref = rest[-2:]
+        key_cols = pl.ds(pl.multiple_of(pl.program_id(0) * HEAD_DIM, HEAD_DIM), HEAD_DIM)
+        place = pl.multiple_of((KV_HEADS + pl.program_id(0)) * HEAD_DIM, HEAD_DIM)
+        d_turned = key_ref[...] + key_more[...].astype(jnp.float32)
+        turned = rope_rows(d_turned, cos_ref[...], -sin_ref[...])
+        d_raw, gain_term = norm_back_rows(raw_ref[...], gain_ref[...], turned)
+        out_ref[:, key_cols] = d_raw.astype(jnp.bfloat16)
+        out_ref[:, pl.ds(place, HEAD_DIM)] = (value_ref[...] + value_more[...].astype(jnp.float32)).astype(
+            jnp.bfloat16
+        )
+
+        @pl.when(pl.program_id(0) == 0)
+        def _():
+            terms_ref[...] = jnp.zeros_like(terms_ref)
+
+        terms_ref[...] += gain_term
+
+    block = lambda offset: pl.BlockSpec((slots, HEAD_DIM), lambda g: (0, offset + g))
+    table = pl.BlockSpec((slots, HEAD_DIM), lambda g: (0, 0))
+    row = pl.BlockSpec((1, HEAD_DIM), lambda g: (0, 0))
+    both_cols = 2 * KV_HEADS * HEAD_DIM
+    return pl.pallas_call(
+        kernel,
+        grid=(KV_HEADS,),
+        out_shape=(
+            jax.ShapeDtypeStruct((slots, both_cols), jnp.bfloat16),
+            jax.ShapeDtypeStruct((1, HEAD_DIM), jnp.float32),
+        ),
+        in_specs=[block(0), block(0), block(0), block(0), block(0), table, table, row]
+        + [pl.BlockSpec(memory_space=pl.ANY)] * len(after),
+        out_specs=(pl.BlockSpec((slots, both_cols), lambda g: (0, 0)), row),
+        compiler_params=pltpu.CompilerParams(vmem_limit_bytes=VMEM_LIMIT),
+        cost_estimate=pl.CostEstimate(
+            flops=20 * slots * KV_HEADS * HEAD_DIM, bytes_accessed=11 * 2**20, transcendentals=0
+        ),
+        name="key_value_back",
+    )(raw, d_key, d_value, key_arrived, value_arrived, cosine, sine, gain, *after)
+
+
+def on_device(
+    tokens,
+    cotangent,
+    lengths,
+    entry_weight,
+    output_weight,
+    gate_weight,
+    down_weight,
+    entry_first,
+    output_first,
+    gate_first,
+    down_first,
+    entry_second,
+    output_second,
+    gate_second,
+    down_second,
+    gains,
+    gains_first,
+    gains_second,
+):
+    seqs, span, width = tokens.shape
+    replicas, members = lax.axis_size("dp"), lax.axis_size("shard")
+    deep = replicas // 4
+    rows_fit = all(
+        w.shape[0] % 16 == 0 for w in (entry_weight, output_weight, gate_weight, down_weight)
+    )
+    if members != 2 or replicas % 8 or deep & (deep - 1) or not rows_fit:
+        return on_device_general(
+            tokens,
+            cotangent,
+            lengths,
+            entry_weight,
+            output_weight,
+            gate_weight,
+            down_weight,
+            entry_first,
+            output_first,
+            gate_first,
+            down_first,
+            entry_second,
+            output_second,
+            gate_second,
+            down_second,
+            gains,
+            gains_first,
+            gains_second,
+        )
+    bf16, f32 = jnp.bfloat16, jnp.float32
+    grid = Grid(replicas)
+    slots = seqs * span
+    query_cols = HEADS * HEAD_DIM
+    gather_sc = lambda w: lax.all_gather(w.astype(bf16), ("dp", "shard"), axis=0, tiled=True)
+    entry_whole, (column, first, second) = gather_rows(grid, entry_weight.astype(bf16))
+    output_whole = gather_sc(output_weight)
+    down_whole = gather_sc(down_weight)
+    gate_whole, _ = gather_rows(
+        grid, tie(gate_weight.astype(bf16), column), after_column=(first, second)
+    )
+
+    g_attn = gains[:D]
+    g_mlp = gains[D : 2 * D]
+    g_query = gains[2 * D : 2 * D + HEAD_DIM]
+    g_key = gains[2 * D + HEAD_DIM :]
+    positions = grid.x * span + jnp.arange(span)
+    cosine, sine = angles(positions)
+    cosine = jnp.concatenate([cosine, cosine], axis=1)
+    sine = jnp.concatenate([-sine, sine], axis=1)
+    cosine, sine = jnp.concatenate([cosine] * seqs), jnp.concatenate([sine] * seqs)
+    live = (positions[None, :] < lengths[:, None]).reshape(slots, 1)
+    shard = grid.x.reshape(1).astype(jnp.int32)
+
+    def dot(left, right):
+        return jnp.dot(left, right, preferred_element_type=f32)
+
+    def dot_turned(left, right):
+        return lax.dot_general(left, right, (((1,), (1,)), ((), ())), preferred_element_type=f32)
+
+    inputs = tokens.astype(f32).reshape(slots, width)
+    normed_one, factor_one = norm_rows(inputs, g_attn)
+    normed_one_low = normed_one.astype(bf16)
+    query_blocks, key_blocks = HEADS // 2, KV_HEADS // 2
+    g_query, g_key = g_query.reshape(1, HEAD_DIM), g_key.reshape(1, HEAD_DIM)
+    key_raw, low = project_heads(
+        normed_one_low, entry_whole, query_blocks, key_blocks, key_blocks, cosine, sine, g_key
+    )
+    other = grid.up_x(low)
+    query_raw, query = project_heads(
+        normed_one_low, entry_whole, 0, query_blocks, 0, cosine, sine, g_query
+    )
+    context = attend(query, low, other, lengths, shard, seqs, span)
+
+    middle = inputs + dot(context, output_whole)
+    normed_two, factor_two = norm_rows(middle, g_mlp)
+    normed_two_low = normed_two.astype(bf16)
+    both = dot(normed_two_low, gate_whole)
+    gate_val, up_val = both[:, :FF], both[:, FF:]
+    sigmoid_val = jax.nn.sigmoid(gate_val)
+    silu_val = gate_val * sigmoid_val
+    hidden = (silu_val * up_val).astype(bf16)
+    back = jnp.where(live, cotangent.reshape(slots, width), jnp.zeros((), bf16))
+    down_part = both_cores(grid, hidden, *halves(grid, back))
+    down_one, down_sent = scatter_one(grid, down_part)
+    d_hidden = dot_turned(back, down_whole)
+    d_gate = d_hidden * up_val * sigmoid_val * (1.0 + gate_val * (1.0 - sigmoid_val))
+    d_up = d_hidden * silu_val
+    d_both = jnp.concatenate([d_gate, d_up], axis=-1).astype(bf16)
+    gate_part = both_cores(grid, normed_two_low, *halves(grid, d_both))
+    gate_one, gate_sent = scatter_one(grid, gate_part)
+    d_normed_two = dot_turned(d_both, gate_whole)
+    d_middle_norm, mlp_gain_terms = norm_back(middle, factor_two, g_mlp, d_normed_two)
+    d_middle = back.astype(f32) + d_middle_norm
+    d_attended = d_middle.astype(bf16)
+    d_context = dot_turned(d_attended, output_whole).astype(bf16)
+    d_query, d_key, d_value, far_key, far_value, query_terms = attend_back(
+        query,
+        low,
+        other,
+        query_raw,
+        d_context,
+        lengths,
+        shard,
+        cosine,
+        sine,
+        g_query,
+        seqs,
+        span,
+        (*down_sent, *gate_sent, *down_one),
+    )
+    key_arrived, value_arrived = grid.down_x(far_key), grid.down_x(far_value)
+    down_two = scatter_two(grid, down_one)
+    output_part = both_cores(grid, context, *halves(grid, d_attended))
+    output_one, output_sent = scatter_one(grid, output_part, d_query)
+    block_out = jnp.where(live, middle + dot(hidden, down_whole), 0.0).astype(bf16)
+    d_key_value, key_terms = key_value_back(
+        key_raw,
+        d_key,
+        d_value,
+        key_arrived,
+        value_arrived,
+        cosine,
+        sine,
+        g_key,
+        (*gate_one, down_two, *output_sent, block_out),
+    )
+    gate_two = scatter_two(grid, gate_one)
+    output_two = scatter_two(grid, output_one)
+    first_core = grid.c == 0
+    entry_part = both_cores(
+        grid,
+        normed_one_low,
+        jnp.where(first_core, d_query, d_key_value),
+        jnp.where(first_core, d_key_value, d_query),
+    )
+    entry_one, entry_sent = scatter_one(grid, entry_part)
+    entry_two = scatter_two(grid, entry_one)
+    owned_down = scatter_three(grid, down_two)
+    owned_gate = scatter_three(grid, gate_two)
+    owned_output = scatter_three(grid, output_two)
+    owned_entry = scatter_three(grid, entry_two)
+    d_normed_one = dot_turned(d_query, entry_whole[:, :query_cols]) + dot_turned(
+        d_key_value, entry_whole[:, query_cols:]
+    )
+    d_inputs_norm, attn_gain_terms = norm_back(inputs, factor_one, g_attn, d_normed_one)
+    token_grad = (d_middle + d_inputs_norm).reshape(seqs, span, width)
+    gain_terms = jnp.concatenate(
+        [
+            jnp.sum(attn_gain_terms, axis=0),
+            jnp.sum(mlp_gain_terms, axis=0),
+            query_terms[0],
+            key_terms[0],
+        ]
+    )
+    grad_gains = sum_all(grid, gain_terms.reshape(-1, HEAD_DIM)).reshape(-1)
+    return (
+        block_out.reshape(seqs, span, width),
+        token_grad,
+        *adam(entry_weight, entry_first, entry_second, owned_entry, RATE_MATRIX, DECAY),
+        *adam(output_weight, output_first, output_second, owned_output, RATE_OUTPUT, DECAY),
+        *adam(gate_weight, gate_first, gate_second, owned_gate, RATE_MATRIX, DECAY),
+        *adam(down_weight, down_first, down_second, owned_down, RATE_MATRIX, DECAY),
+        *adam(gains, gains_first, gains_second, grad_gains, RATE_GAIN, 0.0),
+    )
+
+
 def solution(mesh):
     return jax.shard_map(
         on_device,

time: 1570 us -> 602 us (0.38)
  waiting for transfers between devices: 1130 us -> 230 us
  starting transfers between devices: 0.37 us -> 100 us
  matrix products: 169 us -> 79.8 us
  local copies, waits for them, and re-layouts: 131 us -> 42.4 us
  Pallas kernels: 0 us -> 83.2 us
  blocking collectives: 41.1 us -> 0 us
  other arithmetic: 79.6 us -> 39.5 us
    unnamed x10 -> x2, waiting for transfers between devices: 822 us -> 0.03 us
    all_gather x6 -> x2, waiting for transfers between devices: 304 us -> 0.01 us  [on_device(): lax.all_gather(w.astype(bf16), ('dp', 'shard'), axis=0, tiled=True)]
    ppermute x0 -> x72, waiting for transfers between devices: none -> 230 us  [the longest x69 221 us: send(): return lax.ppermute(values, ('dp', 'shard'), self.pairs(turn))]
    ppermute x0 -> x72, starting transfers between devices: none -> 99.9 us  [the longest x69 93.7 us: send(): return lax.ppermute(values, ('dp', 'shard'), self.pairs(turn))]
    pallas_call x0 -> x11, Pallas kernels: none -> 83.2 us  [the longest x1 27.2 us: attend_back(): pl.pallas_call(kernel, grid=(seqs, KV_HEADS), out_shape=(jax.ShapeDtypeSt...]
    dot_general x17 -> x12, matrix products: 158 us -> 79.8 us  [the longest x5 35.8 us: dot_turned(): lax.dot_general(left, right, (((1,), (1,)), ((), ())), preferred_element_...]
    unnamed x123 -> x181, local copies, waits for them, and re-layouts: 73.7 us -> 28.4 us
    psum x1 -> x0, blocking collectives: 41.1 us -> none  [on_device(): grad_gains = lax.psum(gain_terms, ('dp', 'shard'))]
  transfers between devices with their start and end apart: 9 -> 74, of which waited for: 6 -> 29; matrix products, arithmetic and copies ran while one was open for 17% -> 22% of each run, Pallas kernels for 0% -> 14%
where the time goes in v1:
time: 602 us; the launch traced here: 591 us
  waiting for transfers between devices  230 us (38%)
  starting transfers between devices  100 us (17%)
  Pallas kernels  83.2 us (14%)
  matrix products  79.8 us (13%)
  local copies, waits for them, and re-layouts  42.4 us (7%)
  other arithmetic  39.5 us (7%)
  between operations  15.9 us (3%)
    ppermute x69, waiting for transfers between devices, send(): return lax.ppermute(values, ('dp', 'shard'), self.pairs(turn))  221 us
    ppermute x69, starting transfers between devices, send(): return lax.ppermute(values, ('dp', 'shard'), self.pairs(turn))  93.7 us
    dot_general x5, matrix products, dot_turned(): lax.dot_general(left, right, (((1,), (1,)), ((), ())), preferred_element_...  35.8 us
    unnamed x181, local copies, waits for them, and re-layouts  28.4 us
    pallas_call x1, Pallas kernels, attend_back(): pl.pallas_call(kernel, grid=(seqs, KV_HEADS), out_shape=(jax.ShapeDtypeSt...  27.2 us
    dot_general x4, matrix products, both_cores(): lax.dot_general(left_all, right_all, (((0,), (0,)), ((), ())), preferred_...  24.7 us
    dot_general x3, matrix products, dot(): return jnp.dot(left, right, preferred_element_type=f32)  19.3 us
    pallas_call x2, Pallas kernels, project_heads(): pl.pallas_call(kernel, grid=(blocks,), out_shape=(jax.ShapeDtypeStruct((s...  17.8 us
  transfers between devices with their start and end apart: 74, of which 29 were waited for; matrix products, arithmetic and copies ran while one was open for 22% of the time, Pallas kernels for 14%

profile of v1, /device:TPU:0, one launch (start us, length us, event | category | flops | bytes accessed | tf_op | source)
XLA Modules:
  0.0 591.1 jit_solution(3551903778963188615)
XLA Ops:
  19.7 4.5 collective-permute-done
  24.2 12.2 %collective-permute-done.1 = bf16[32,4096]{1,0:T(8,128)(2,1)S(1)} collective-permute-done((bf16[32,4096]{1,0:T(8,128)(2,1)S(1)}, bf16[32,4096]{1,0:T(8,128)(2,1)S(1)}, u32[]{:S(2)}, u32[]{:S(2)}) %collective-permute-start.1) | collective-permute-done | bytes 262176 | tf_op jit(solution)/shard_map/ppermute | solution.py:104
  43.1 7.2 %collective-permute-start.13 = (bf16[32,6144]{1,0:T(8,128)(2,1)}, bf16[32,6144]{1,0:T(8,128)(2,1)S(1)}, u32[]{:S(2)}, u32[]{:S(2)}) collective-permute-start(bf16[32,6144]{1,0:T(8,128)(2,1)} %tie.4), channel_id=1, source_target_pairs={{0,8},{1,9},{2,10},{3,11},{4,12},{5,13},{6,14},{7,15},{8,16},{9,17... | collective-permute-start | bytes 1179656 | tf_op jit(solution)/shard_map/ppermute | solution.py:104
  52.8 14.6 %collective-permute-done.3.refs_1_ = bf16[4,32,4096]{2,1,0:T(8,128)(2,1)S(1)} collective-permute-done((bf16[4,32,4096]{2,1,0:T(8,128)(2,1)}, bf16[4,32,4096]{2,1,0:T(8,128)(2,1)S(1)}, u32[]{:S(2)}, u32[]{:S(2)}) %collective-permute-start.3) | collective-permute-done | bytes 1048608 | tf_op jit(solution)/shard_map/ppermute | solution.py:104
  72.1 9.1 %collective-permute-done.14 = bf16[32,6144]{1,0:T(8,128)(2,1)S(1)} collective-permute-done((bf16[32,6144]{1,0:T(8,128)(2,1)}, bf16[32,6144]{1,0:T(8,128)(2,1)S(1)}, u32[]{:S(2)}, u32[]{:S(2)}) %collective-permute-start.14) | collective-permute-done | bytes 393248 | tf_op jit(solution)/shard_map/ppermute | solution.py:104
  94.4 6.4 %project_heads.3 = (f32[512,1024]{1,0:T(8,128)S(1)}, bf16[512,2048]{1,0:T(8,128)(2,1)S(1)}) custom-call(bf16[512,1024]{1,0:T(8,128)(2,1)S(1)} %copy-done.25, bf16[1024,4096]{1,0:T(8,128)(2,1)S(1)} %bitcast.271, f32[512,128]{1,0:T(8,128)S(1)} %get-tuple-element.120.cos_ref, f32[512,128]{1,0:T(8,128)S(1)} %get-tuple-element.121.sin_ref, ...), custom_call_target="tpu_custom_call" | custom-call | flops 8589934592 | bytes 12582912 | tf_op jit(solution)/shard_map/project_heads/pallas_call | solution.py:561
  105.8 20.3 %collective-permute-done.16.refs_1_ = bf16[4,32,6144]{2,1,0:T(8,128)(2,1)S(1)} collective-permute-done((bf16[4,32,6144]{2,1,0:T(8,128)(2,1)}, bf16[4,32,6144]{2,1,0:T(8,128)(2,1)S(1)}, u32[]{:S(2)}, u32[]{:S(2)}) %collective-permute-start.16) | collective-permute-done | bytes 1572896 | tf_op jit(solution)/shard_map/ppermute | solution.py:104
  132.9 17.7 %collective-permute-done.18.refs_3_ = bf16[2,32,6144]{2,1,0:T(8,128)(2,1)S(1)} collective-permute-done((bf16[2,32,6144]{2,1,0:T(8,128)(2,1)}, bf16[2,32,6144]{2,1,0:T(8,128)(2,1)S(1)}, u32[]{:S(2)}, u32[]{:S(2)}) %collective-permute-start.18) | collective-permute-done | bytes 786464 | tf_op jit(solution)/shard_map/ppermute | solution.py:104
  153.4 50.7 %collective-permute-done.19.refs_4_ = bf16[2,32,6144]{2,1,0:T(8,128)(2,1)} collective-permute-done((bf16[2,32,6144]{2,1,0:T(8,128)(2,1)}, bf16[2,32,6144]{2,1,0:T(8,128)(2,1)}, u32[]{:S(2)}, u32[]{:S(2)}) %collective-permute-start.19) | collective-permute-done | bytes 786464 | tf_op jit(solution)/shard_map/ppermute | solution.py:104
  204.6 11.3 %project_heads.2 = (f32[512,2048]{1,0:T(8,128)S(1)}, bf16[512,2048]{1,0:T(8,128)(2,1)S(1)}) custom-call(bf16[512,1024]{1,0:T(8,128)(2,1)S(1)} %copy-done.26, bf16[1024,4096]{1,0:T(8,128)(2,1)} %bitcast.272, f32[512,128]{1,0:T(8,128)S(1)} %get-tuple-element.120.cos_ref, f32[512,128]{1,0:T(8,128)S(1)} %get-tuple-element.121.sin_ref, ...), custom_call_target="tpu_custom_call" | custom-call | flops 8589934592 | bytes 12582912 | tf_op jit(solution)/shard_map/project_heads/pallas_call | solution.py:561
  217.9 16.5 %attend.1 = bf16[512,2048]{1,0:T(8,128)(2,1)} custom-call(s32[2]{0:T(128)S(1)} %copy-done.28, s32[1]{0:T(128)} %bitcast.1.place_ref, bf16[512,2048]{1,0:T(8,128)(2,1)S(1)} %get-tuple-element.29.query_ref, bf16[512,2048]{1,0:T(8,128)(2,1)S(1)} %get-tuple-element.30.key_ref.value_ref, bf16[512,2048]{1,0:T(8,128)(2,1)S(1)} %get-tuple-element.30.key_ref.value_ref, ...), custom_call_target="tpu_custom_call" | custom-call | flops 2147483648 | bytes 12582912 | tf_op jit(solution)/shard_map/attend/pallas_call | solution.py:626
  235.1 11.1 %place_blocks.3 = bf16[32,32,6144]{2,1,0:T(8,128)(2,1)S(1)} custom-call(s32[4]{0:T(128)S(1)} %pad_add_fusion.place_ref, bf16[4,32,6144]{2,1,0:T(8,128)(2,1)S(1)} %copy-done.3, bf16[4,32,6144]{2,1,0:T(8,128)(2,1)S(1)} %copy-done.12, bf16[4,32,6144]{2,1,0:T(8,128)(2,1)S(1)} %copy-done.14, bf16[2,32,6144]{2,1,0:T(8,128)(2,1)S(1)} %collective-permute-done.18.refs_3_, ...), custom_call_target="tpu_custom_call" | custom-call | bytes 25165824 | tf_op jit(solution)/shard_map/place_blocks/pallas_call | solution.py:169
  246.1 4.6 copy-done.4
  250.7 5.7 multiply_reduce_fusion.2
  257.6 9.2 %fusion.152 = f32[512,6144]{1,0:T(8,128)} fusion(bf16[512,1024]{1,0:T(8,128)(2,1)S(1)} %multiply_convert_fusion.3, bf16[1024,6144]{1,0:T(8,128)(2,1)S(1)} %bitcast.270), kind=kOutput, calls=%fused_computation.289 | convolution fusion | flops 6442450944 | bytes 26214400 | tf_op jit(solution)/shard_map/dot_general | solution.py:894
  266.8 13.1 %multiply_convert_fusion.1 = (bf16[512,3072]{1,0:T(8,128)(2,1)}, bf16[512,3072]{1,0:T(8,128)(2,1)}, bf16[512,3072]{1,0:T(8,128)(2,1)}) fusion(f32[512,6144]{1,0:T(8,128)} %fusion.152, bf16[512,1024]{1,0:T(8,128)(2,1)} %copy-done.48, bf16[3072,1024]{1,0:T(8,128)(2,1)} %all-gather.5.cloned.1.call-done), kind=kOutput, calls=%fused_computation.15 | convolution fusion | flops 3244818432 | bytes 29360128 | tf_op jit(solution)/shard_map/dot_general | solution.py:897
  279.9 13.9 %multiply_reduce_fusion = (f32[1024]{0:T(1024)S(1)}, f32[512]{0:T(512)S(1)}, f32[512,1024]{1,0:T(8,128)}) fusion(f32[512,1024]{1,0:T(8,128)S(1)} %get-tuple-element.117, f32[512]{0:T(512)S(1)} %add_rsqrt_fusion, f32[1024]{0:T(1024)S(1)} %get-tuple-element.109, bf16[1024,6144]{1,0:T(8,128)(2,1)} %bitcast.269, bf16[512,3072]{1,0:T(8,128)(2,1)} %get-tuple-element.61, ...), kind=kOutput, calls=%fused_computation.74 | convolution fusion | flops 6458178048 | bytes 23080960 | tf_op jit(solution)/shard_map/dot_general | solution.py:897
  310.5 4.6 fusion.35
  318.2 4.8 fusion.13
  326.4 9.2 %fusion.10 = bf16[1024,3072]{1,0:T(8,128)(2,1)S(1)} fusion(bf16[512,3072]{1,0:T(8,128)(2,1)} %collective-permute-done.28, bf16[512,3072]{1,0:T(8,128)(2,1)S(1)} %get-tuple-element.65, bf16[512,1024]{1,0:T(8,128)(2,1)S(1)} %collective-permute-done.27, bf16[512,1024]{1,0:T(8,128)(2,1)S(1)} %copy-done.60), kind=kOutput, calls=%fused_computation.19 | convolution fusion | flops 6462373888 | bytes 14680064 | tf_op jit(solution)/shard_map/dot_general | solution.py:213
  340.7 5.3 collective-permute-done.29
  348.9 27.2 %attend_back.1 = (bf16[512,2048]{1,0:T(8,128)(2,1)S(1)}, f32[512,1024]{1,0:T(8,128)S(1)}, f32[512,1024]{1,0:T(8,128)}, bf16[512,1024]{1,0:T(8,128)(2,1)S(1)}, bf...) custom-call(s32[2]{0:T(128)S(1)} %copy-done.28, s32[1]{0:T(128)} %bitcast.1.place_ref, bf16[512,2048]{1,0:T(8,128)(2,1)} %copy-done.8, ...), custom_call_target="tpu_custom_call" | custom-call | flops 5368709120 | bytes 25165824 | tf_op jit(solution)/shard_map/attend_back/pallas_call | solution.py:733
  389.1 13.0 %collective-permute-start.63 = (bf16[2,96,512]{2,1,0:T(8,128)(2,1)S(1)}, bf16[2,96,512]{2,1,0:T(8,128)(2,1)S(1)}, u32[]{:S(2)}, u32[]{:S(2)}) collective-permute-start(bf16[2,96,512]{2,1,0:T(8,128)(2,1)S(1)} %get-tuple-element.95), channel_id=1, source_target_pairs={{0,8},{1,9},{2,10},{3,11},{4,12},{5,13},{6,14},{7,15},{8,16},{9,17... | collective-permute-start | bytes 589832 | tf_op jit(solution)/shard_map/ppermute | solution.py:104
  405.1 7.7 %collective-permute-start.65 = (bf16[2,96,512]{2,1,0:T(8,128)(2,1)S(1)}, bf16[2,96,512]{2,1,0:T(8,128)(2,1)S(1)}, u32[]{:S(2)}, u32[]{:S(2)}) collective-permute-start(bf16[2,96,512]{2,1,0:T(8,128)(2,1)S(1)} %get-tuple-element.97), channel_id=1, source_target_pairs={{0,24},{1,25},{2,26},{3,27},{4,28},{5,29},{6,30},{7,31},{8,0},{9,1... | collective-permute-start | bytes 589832 | tf_op jit(solution)/shard_map/ppermute | solution.py:104
  426.3 28.2 %collective-permute-done.52 = bf16[4,64,512]{2,1,0:T(8,128)(2,1)S(1)} collective-permute-done((bf16[4,64,512]{2,1,0:T(8,128)(2,1)S(1)}, bf16[4,64,512]{2,1,0:T(8,128)(2,1)S(1)}, u32[]{:S(2)}, u32[]{:S(2)}) %collective-permute-start.52) | collective-permute-done | bytes 262176 | tf_op jit(solution)/shard_map/ppermute | solution.py:104
  470.5 9.5 %collective-permute-done.32.value_more = bf16[512,1024]{1,0:T(8,128)(2,1)S(1)} collective-permute-done((bf16[512,1024]{1,0:T(8,128)(2,1)S(1)}, bf16[512,1024]{1,0:T(8,128)(2,1)S(1)}, u32[]{:S(2)}, u32[]{:S(2)}) %collective-permute-start.32) | collective-permute-done | bytes 1048608 | tf_op jit(solution)/shard_map/ppermute | solution.py:124
  483.5 6.8 %key_value_back.1 = (bf16[512,2048]{1,0:T(8,128)(2,1)S(1)}, f32[1,128]{1,0:T(1,128)S(1)}) custom-call(f32[512,1024]{1,0:T(8,128)S(1)} %copy-done.16, f32[512,1024]{1,0:T(8,128)} %copy-done.17, f32[512,1024]{1,0:T(8,128)} %get-tuple-element.35.value_ref, bf16[512,1024]{1,0:T(8,128)(2,1)S(1)} %copy-done.22, bf16[512,1024]{1,0:T(8,128)(2,1)S(1)} %copy-done.24, ...), custom_call_target="tpu_custom_call" | custom-call | flops 10485760 | bytes 11534336 | tf_op jit(solution)/shard_map/key_value_back/pallas_call | solution.py:804
  514.7 6.1 %fusion.28 = bf16[1024,2048]{1,0:T(8,128)(2,1)S(1)} fusion(bf16[512,2048]{1,0:T(8,128)(2,1)S(1)} %collective-permute-done.40, bf16[512,2048]{1,0:T(8,128)(2,1)S(1)} %get-tuple-element.69, bf16[512,1024]{1,0:T(8,128)(2,1)} %collective-permute-done.39, bf16[512,1024]{1,0:T(8,128)(2,1)S(1)} %copy-done.27), kind=kOutput, calls=%fused_computation.33 | convolution fusion | flops 4309647360 | bytes 10485760 | tf_op jit(solution)/shard_map/dot_general | solution.py:213
  523.2 5.3 collective-permute-done.57
  535.1 11.6 %collective-permute-done.43 = bf16[4,2,32,2048]{3,2,1,0:T(8,128)(2,1)S(1)} collective-permute-done((bf16[4,2,32,2048]{3,2,1,0:T(8,128)(2,1)S(1)}, bf16[4,2,32,2048]{3,2,1,0:T(8,128)(2,1)S(1)}, u32[]{:S(2)}, u32[]{:S(2)}) %collective-permute-start.43) | collective-permute-done | bytes 1048608 | tf_op jit(solution)/shard_map/ppermute | solution.py:104
  559.3 5.1 collective-permute-start.45
  571.2 7.7 %collective-permute-done.46 = bf16[2,32,2048]{2,1,0:T(8,128)(2,1)S(1)} collective-permute-done((bf16[2,32,2048]{2,1,0:T(8,128)(2,1)S(1)}, bf16[2,32,2048]{2,1,0:T(8,128)(2,1)S(1)}, u32[]{:S(2)}, u32[]{:S(2)}) %collective-permute-start.46) | collective-permute-done | bytes 262176 | tf_op jit(solution)/shard_map/ppermute | solution.py:104
  (422 shorter events, 195.1 us)
Async XLA Ops:
  7.2 243.5 %all-gather.3.cloned.1.call-start = ((), (), s32[]{:S(2)}) async-start(), calls=%async_computation | async-start | bytes 4325376 | tf_op jit(solution)/shard_map/all_gather | solution.py:873
  9.0 257.8 %all-gather.5.cloned.1.call-start = ((), (), s32[]{:S(2)}) async-start(), calls=%async_computation.1 | async-start | bytes 6488064 | tf_op jit(solution)/shard_map/all_gather | solution.py:873
  38.4 28.9 %collective-permute-start.3 = (bf16[4,32,4096]{2,1,0:T(8,128)(2,1)}, bf16[4,32,4096]{2,1,0:T(8,128)(2,1)S(1)}, u32[]{:S(2)}, u32[]{:S(2)}) collective-permute-start(bf16[4,32,4096]{2,1,0:T(8,128)(2,1)} %pad_maximum_fusion.4.refs_0_.refs_1_), channel_id=1, source_target_pairs={{0,1},{1,0},{2,3},{3,2},{4,5},{5,4},{6,7},{7,6},{8,9},{9,8},{10,11... | collective-permute-start | bytes 3145736 | tf_op jit(solution)/shard_map/ppermute | solution.py:104
  40.0 29.0 %collective-permute-start.4 = (bf16[4,32,4096]{2,1,0:T(8,128)(2,1)}, bf16[4,32,4096]{2,1,0:T(8,128)(2,1)S(1)}, u32[]{:S(2)}, u32[]{:S(2)}) collective-permute-start(bf16[4,32,4096]{2,1,0:T(8,128)(2,1)} %pad_maximum_fusion.4.refs_0_.refs_1_), channel_id=1, source_target_pairs={{0,4},{1,5},{2,6},{3,7},{4,0},{5,1},{6,2},{7,3},{8,12},{9,13},{10,... | collective-permute-start | bytes 3145736 | tf_op jit(solution)/shard_map/ppermute | solution.py:104
  43.1 27.9 %collective-permute-start.13 = (bf16[32,6144]{1,0:T(8,128)(2,1)}, bf16[32,6144]{1,0:T(8,128)(2,1)S(1)}, u32[]{:S(2)}, u32[]{:S(2)}) collective-permute-start(bf16[32,6144]{1,0:T(8,128)(2,1)} %tie.4), channel_id=1, source_target_pairs={{0,8},{1,9},{2,10},{3,11},{4,12},{5,13},{6,14},{7,15},{8,16},{9,17... | collective-permute-start | bytes 1179656 | tf_op jit(solution)/shard_map/ppermute | solution.py:104
  50.3 30.9 %collective-permute-start.14 = (bf16[32,6144]{1,0:T(8,128)(2,1)}, bf16[32,6144]{1,0:T(8,128)(2,1)S(1)}, u32[]{:S(2)}, u32[]{:S(2)}) collective-permute-start(bf16[32,6144]{1,0:T(8,128)(2,1)} %tie.4), channel_id=1, source_target_pairs={{0,16},{1,17},{2,18},{3,19},{4,20},{5,21},{6,22},{7,23},{8,24},{9,... | collective-permute-start | bytes 1179656 | tf_op jit(solution)/shard_map/ppermute | solution.py:104
  51.9 29.3 %collective-permute-start.15 = (bf16[32,6144]{1,0:T(8,128)(2,1)}, bf16[32,6144]{1,0:T(8,128)(2,1)}, u32[]{:S(2)}, u32[]{:S(2)}) collective-permute-start(bf16[32,6144]{1,0:T(8,128)(2,1)} %tie.4), channel_id=1, source_target_pairs={{0,24},{1,25},{2,26},{3,27},{4,28},{5,29},{6,30},{7,31},{8,0},{9,1... | collective-permute-start | bytes 1179656 | tf_op jit(solution)/shard_map/ppermute | solution.py:104
  86.8 39.3 %collective-permute-start.16 = (bf16[4,32,6144]{2,1,0:T(8,128)(2,1)}, bf16[4,32,6144]{2,1,0:T(8,128)(2,1)S(1)}, u32[]{:S(2)}, u32[]{:S(2)}) collective-permute-start(bf16[4,32,6144]{2,1,0:T(8,128)(2,1)} %tie.5.refs_0_), channel_id=1, source_target_pairs={{0,1},{1,0},{2,3},{3,2},{4,5},{5,4},{6,7},{7,6},{8,9},{9,8},{10,11... | collective-permute-start | bytes 4718600 | tf_op jit(solution)/shard_map/ppermute | solution.py:104
  89.5 38.7 %collective-permute-start.17 = (bf16[4,32,6144]{2,1,0:T(8,128)(2,1)}, bf16[4,32,6144]{2,1,0:T(8,128)(2,1)S(1)}, u32[]{:S(2)}, u32[]{:S(2)}) collective-permute-start(bf16[4,32,6144]{2,1,0:T(8,128)(2,1)} %tie.5.refs_0_), channel_id=1, source_target_pairs={{0,4},{1,5},{2,6},{3,7},{4,0},{5,1},{6,2},{7,3},{8,12},{9,13},{10,... | collective-permute-start | bytes 4718600 | tf_op jit(solution)/shard_map/ppermute | solution.py:104
  102.2 101.9 %collective-permute-start.12 = (bf16[512,2048]{1,0:T(8,128)(2,1)S(1)}, bf16[512,2048]{1,0:T(8,128)(2,1)}, u32[]{:S(2)}, u32[]{:S(2)}) collective-permute-start(bf16[512,2048]{1,0:T(8,128)(2,1)S(1)} %get-tuple-element.30.key_ref.value_ref), channel_id=1, source_target_pairs={{0,1},{2,3},{4,5},{6,7},{8,9},{10,11},{12,13},{14,15},{16,17},{18,... | collective-permute-start | bytes 6291464 | tf_op jit(solution)/shard_map/ppermute | solution.py:120
  130.2 73.8 %collective-permute-start.19 = (bf16[2,32,6144]{2,1,0:T(8,128)(2,1)}, bf16[2,32,6144]{2,1,0:T(8,128)(2,1)}, u32[]{:S(2)}, u32[]{:S(2)}) collective-permute-start(bf16[2,32,6144]{2,1,0:T(8,128)(2,1)} %slice.83), channel_id=1, source_target_pairs={{0,1},{1,0},{2,3},{3,2},{4,5},{5,4},{6,7},{7,6},{8,9},{9,8},{10,11... | collective-permute-start | bytes 2359304 | tf_op jit(solution)/shard_map/ppermute | solution.py:104
  132.4 102.1 %collective-permute-start.20 = (bf16[4,32,6144]{2,1,0:T(8,128)(2,1)}, bf16[4,32,6144]{2,1,0:T(8,128)(2,1)}, u32[]{:S(2)}, u32[]{:S(2)}) collective-permute-start(bf16[4,32,6144]{2,1,0:T(8,128)(2,1)} %tie.5.refs_0_), channel_id=1, source_target_pairs={{0,2},{1,3},{2,0},{3,1},{4,6},{5,7},{6,4},{7,5},{8,10},{9,11},{10,... | collective-permute-start | bytes 4718600 | tf_op jit(solution)/shard_map/ppermute | solution.py:104
  132.4 102.7 %collective-permute-start.21 = (bf16[4,32,6144]{2,1,0:T(8,128)(2,1)}, bf16[4,32,6144]{2,1,0:T(8,128)(2,1)}, u32[]{:S(2)}, u32[]{:S(2)}) collective-permute-start(bf16[4,32,6144]{2,1,0:T(8,128)(2,1)} %copy-done.11), channel_id=1, source_target_pairs={{0,2},{1,3},{2,0},{3,1},{4,6},{5,7},{6,4},{7,5},{8,10},{9,11},{10,... | collective-permute-start | bytes 4718600 | tf_op jit(solution)/shard_map/ppermute | solution.py:104
  150.6 84.5 %collective-permute-start.22 = (bf16[4,32,6144]{2,1,0:T(8,128)(2,1)}, bf16[4,32,6144]{2,1,0:T(8,128)(2,1)}, u32[]{:S(2)}, u32[]{:S(2)}) collective-permute-start(bf16[4,32,6144]{2,1,0:T(8,128)(2,1)} %copy-done.13), channel_id=1, source_target_pairs={{0,2},{1,3},{2,0},{3,1},{4,6},{5,7},{6,4},{7,5},{8,10},{9,11},{10,... | collective-permute-start | bytes 4718600 | tf_op jit(solution)/shard_map/ppermute | solution.py:104
  204.1 30.4 %collective-permute-start.23 = (bf16[2,32,6144]{2,1,0:T(8,128)(2,1)S(1)}, bf16[2,32,6144]{2,1,0:T(8,128)(2,1)S(1)}, u32[]{:S(2)}, u32[]{:S(2)}) collective-permute-start(bf16[2,32,6144]{2,1,0:T(8,128)(2,1)S(1)} %collective-permute-done.18.refs_3_), channel_id=1, source_target_pairs={{0,2},{1,3},{2,0},{3,1},{4,6},{5,7},{6,4},{7,5},{8,10},{9,11},{10,... | collective-permute-start | bytes 2359304 | tf_op jit(solution)/shard_map/ppermute | solution.py:104
  204.1 30.9 %collective-permute-start.24 = (bf16[2,32,6144]{2,1,0:T(8,128)(2,1)}, bf16[2,32,6144]{2,1,0:T(8,128)(2,1)S(1)}, u32[]{:S(2)}, u32[]{:S(2)}) collective-permute-start(bf16[2,32,6144]{2,1,0:T(8,128)(2,1)} %collective-permute-done.19.refs_4_), channel_id=1, source_target_pairs={{0,2},{1,3},{2,0},{3,1},{4,6},{5,7},{6,4},{7,5},{8,10},{9,11},{10,... | collective-permute-start | bytes 2359304 | tf_op jit(solution)/shard_map/ppermute | solution.py:104
  234.4 83.8 %collective-permute-start.26 = (bf16[512,512]{1,0:T(8,128)(2,1)}, bf16[512,512]{1,0:T(8,128)(2,1)}, u32[]{:S(2)}, u32[]{:S(2)}) collective-permute-start(bf16[512,512]{1,0:T(8,128)(2,1)} %get-tuple-element.94), channel_id=1, source_target_pairs={{0,2},{1,3},{2,0},{3,1},{4,6},{5,7},{6,4},{7,5},{8,10},{9,11},{10,... | collective-permute-start | bytes 1572872 | tf_op jit(solution)/shard_map/ppermute | solution.py:104
  234.5 75.9 %collective-permute-start.37 = (bf16[512,2048]{1,0:T(8,128)(2,1)}, bf16[512,2048]{1,0:T(8,128)(2,1)}, u32[]{:S(2)}, u32[]{:S(2)}) collective-permute-start(bf16[512,2048]{1,0:T(8,128)(2,1)} %attend.1), channel_id=1, source_target_pairs={{0,2},{1,3},{2,0},{3,1},{4,6},{5,7},{6,4},{7,5},{8,10},{9,11},{10,... | collective-permute-start | bytes 6291464 | tf_op jit(solution)/shard_map/ppermute | solution.py:104
  293.8 24.4 %collective-permute-start.25 = (bf16[512,3072]{1,0:T(8,128)(2,1)}, bf16[512,3072]{1,0:T(8,128)(2,1)S(1)}, u32[]{:S(2)}, u32[]{:S(2)}) collective-permute-start(bf16[512,3072]{1,0:T(8,128)(2,1)} %get-tuple-element.62), channel_id=1, source_target_pairs={{0,2},{1,3},{2,0},{3,1},{4,6},{5,7},{6,4},{7,5},{8,10},{9,11},{10,... | collective-permute-start | bytes 9437192 | tf_op jit(solution)/shard_map/ppermute | solution.py:104
  301.8 24.6 %collective-permute-start.28 = (bf16[512,3072]{1,0:T(8,128)(2,1)S(1)}, bf16[512,3072]{1,0:T(8,128)(2,1)}, u32[]{:S(2)}, u32[]{:S(2)}) collective-permute-start(bf16[512,3072]{1,0:T(8,128)(2,1)S(1)} %get-tuple-element.66), channel_id=1, source_target_pairs={{0,2},{1,3},{2,0},{3,1},{4,6},{5,7},{6,4},{7,5},{8,10},{9,11},{10,... | collective-permute-start | bytes 9437192 | tf_op jit(solution)/shard_map/ppermute | solution.py:104
  336.5 121.0 %collective-permute-start.34 = (bf16[4,2,32,3072]{3,2,1,0:T(8,128)(2,1)S(1)}, bf16[4,2,32,3072]{3,2,1,0:T(8,128)(2,1)}, u32[]{:S(2)}, u32[]{:S(2)}) collective-permute-start(bf16[4,2,32,3072]{3,2,1,0:T(8,128)(2,1)S(1)} %dynamic-slice_bitcast_fusion.rest_3_), channel_id=1, source_target_pairs={{0,1},{1,0},{2,3},{3,2},{4,5},{5,4},{6,7},{7,6},{8,9},{9,8},{10,11... | collective-permute-start | bytes 4718600 | tf_op jit(solution)/shard_map/ppermute | solution.py:104
  348.3 38.4 %collective-permute-start.35 = (bf16[4,96,512]{2,1,0:T(8,128)(2,1)}, bf16[4,96,512]{2,1,0:T(8,128)(2,1)}, u32[]{:S(2)}, u32[]{:S(2)}) collective-permute-start(bf16[4,96,512]{2,1,0:T(8,128)(2,1)} %dynamic-slice_bitcast_fusion.11), channel_id=1, source_target_pairs={{0,1},{1,0},{2,3},{3,2},{4,5},{5,4},{6,7},{7,6},{8,9},{9,8},{10,11... | collective-permute-start | bytes 1179656 | tf_op jit(solution)/shard_map/ppermute | solution.py:104
  348.6 39.2 %collective-permute-start.36 = (bf16[4,96,512]{2,1,0:T(8,128)(2,1)}, bf16[4,96,512]{2,1,0:T(8,128)(2,1)}, u32[]{:S(2)}, u32[]{:S(2)}) collective-permute-start(bf16[4,96,512]{2,1,0:T(8,128)(2,1)} %dynamic-slice_bitcast_fusion.10), channel_id=1, source_target_pairs={{0,4},{1,5},{2,6},{3,7},{4,0},{5,1},{6,2},{7,3},{8,12},{9,13},{10,... | collective-permute-start | bytes 1179656 | tf_op jit(solution)/shard_map/ppermute | solution.py:104
  384.7 36.5 %collective-permute-start.49 = (bf16[4,2,64,512]{3,2,0,1:T(8,128)(2,1)S(1)}, bf16[4,2,64,512]{3,2,0,1:T(8,128)(2,1)S(1)}, u32[]{:S(2)}, u32[]{:S(2)}) collective-permute-start(bf16[4,2,64,512]{3,2,0,1:T(8,128)(2,1)S(1)} %copy.66), channel_id=1, source_target_pairs={{0,4},{1,5},{2,6},{3,7},{4,0},{5,1},{6,2},{7,3},{8,12},{9,13},{10,... | collective-permute-start | bytes 1572872 | tf_op jit(solution)/shard_map/ppermute | solution.py:104
  413.1 43.0 %collective-permute-start.33 = (bf16[4,2,32,3072]{3,2,0,1:T(8,128)(2,1)S(1)}, bf16[4,2,32,3072]{3,2,0,1:T(8,128)(2,1)S(1)}, u32[]{:S(2)}, u32[]{:S(2)}) collective-permute-start(bf16[4,2,32,3072]{3,2,0,1:T(8,128)(2,1)S(1)} %bitcast.292), channel_id=1, source_target_pairs={{0,4},{1,5},{2,6},{3,7},{4,0},{5,1},{6,2},{7,3},{8,12},{9,13},{10,... | collective-permute-start | bytes 4718600 | tf_op jit(solution)/shard_map/ppermute | solution.py:104
  417.7 51.7 %collective-permute-start.31 = (bf16[512,1024]{1,0:T(8,128)(2,1)S(1)}, bf16[512,1024]{1,0:T(8,128)(2,1)S(1)}, u32[]{:S(2)}, u32[]{:S(2)}) collective-permute-start(bf16[512,1024]{1,0:T(8,128)(2,1)S(1)} %copy-done.32), channel_id=1, source_target_pairs={{1,0},{3,2},{5,4},{7,6},{9,8},{11,10},{13,12},{15,14},{17,16},{19,... | collective-permute-start | bytes 3145736 | tf_op jit(solution)/shard_map/ppermute | solution.py:124
  419.4 35.1 %collective-permute-start.52 = (bf16[4,64,512]{2,1,0:T(8,128)(2,1)S(1)}, bf16[4,64,512]{2,1,0:T(8,128)(2,1)S(1)}, u32[]{:S(2)}, u32[]{:S(2)}) collective-permute-start(bf16[4,64,512]{2,1,0:T(8,128)(2,1)S(1)} %dynamic-slice_bitcast_fusion.12), channel_id=1, source_target_pairs={{0,4},{1,5},{2,6},{3,7},{4,0},{5,1},{6,2},{7,3},{8,12},{9,13},{10,... | collective-permute-start | bytes 786440 | tf_op jit(solution)/shard_map/ppermute | solution.py:104
  422.7 33.1 %collective-permute-start.50 = (bf16[4,64,512]{2,1,0:T(8,128)(2,1)S(1)}, bf16[4,64,512]{2,1,0:T(8,128)(2,1)S(1)}, u32[]{:S(2)}, u32[]{:S(2)}) collective-permute-start(bf16[4,64,512]{2,1,0:T(8,128)(2,1)S(1)} %dynamic-slice_bitcast_fusion.13), channel_id=1, source_target_pairs={{0,1},{1,0},{2,3},{3,2},{4,5},{5,4},{6,7},{7,6},{8,9},{9,8},{10,11... | collective-permute-start | bytes 786440 | tf_op jit(solution)/shard_map/ppermute | solution.py:104
  454.5 25.5 %collective-permute-start.32 = (bf16[512,1024]{1,0:T(8,128)(2,1)S(1)}, bf16[512,1024]{1,0:T(8,128)(2,1)S(1)}, u32[]{:S(2)}, u32[]{:S(2)}) collective-permute-start(bf16[512,1024]{1,0:T(8,128)(2,1)S(1)} %copy-done.30), channel_id=1, source_target_pairs={{1,0},{3,2},{5,4},{7,6},{9,8},{11,10},{13,12},{15,14},{17,16},{19,... | collective-permute-start | bytes 3145736 | tf_op jit(solution)/shard_map/ppermute | solution.py:124
  464.7 50.0 %collective-permute-start.39 = (bf16[512,1024]{1,0:T(8,128)(2,1)S(1)}, bf16[512,1024]{1,0:T(8,128)(2,1)}, u32[]{:S(2)}, u32[]{:S(2)}) collective-permute-start(bf16[512,1024]{1,0:T(8,128)(2,1)S(1)} %copy-done.27), channel_id=1, source_target_pairs={{0,2},{1,3},{2,0},{3,1},{4,6},{5,7},{6,4},{7,5},{8,10},{9,11},{10,... | collective-permute-start | bytes 3145736 | tf_op jit(solution)/shard_map/ppermute | solution.py:104
  467.6 45.8 %collective-permute-start.58 = (bf16[4,32,3072]{2,1,0:T(8,128)(2,1)}, bf16[4,32,3072]{2,1,0:T(8,128)(2,1)}, u32[]{:S(2)}, u32[]{:S(2)}) collective-permute-start(bf16[4,32,3072]{2,1,0:T(8,128)(2,1)} %dynamic-slice_bitcast_fusion.2), channel_id=1, source_target_pairs={{0,4},{1,5},{2,6},{3,7},{4,0},{5,1},{6,2},{7,3},{8,12},{9,13},{10,... | collective-permute-start | bytes 2359304 | tf_op jit(solution)/shard_map/ppermute | solution.py:104
  521.2 25.5 %collective-permute-start.43 = (bf16[4,2,32,2048]{3,2,1,0:T(8,128)(2,1)S(1)}, bf16[4,2,32,2048]{3,2,1,0:T(8,128)(2,1)S(1)}, u32[]{:S(2)}, u32[]{:S(2)}) collective-permute-start(bf16[4,2,32,2048]{3,2,1,0:T(8,128)(2,1)S(1)} %dynamic-slice_bitcast_fusion.1), channel_id=1, source_target_pairs={{0,1},{1,0},{2,3},{3,2},{4,5},{5,4},{6,7},{7,6},{8,9},{9,8},{10,11... | collective-permute-start | bytes 3145736 | tf_op jit(solution)/shard_map/ppermute | solution.py:104
  (130 other events, 1569.6 us)
Sparse Core Ops, SparseCore 0:
  11.6 91.8 all-gather.2
  106.9 79.3 all-gather.4
